TPU v7x, 32 devices: a whole 2x2x4 slice. The times are simulated.
32 devices in a mesh: sfc: 32 (over z, y, x, core).
Axes of the slice: x: 2, y: 2, z: 4, core: 2. Of those that a mesh axis runs over, the one named last changes fastest.
Arguments:
- fraction: float32 [256, 4096], P('sfc'), may hold values from 0 to 1
- centroid: float32 [256, 3, 4096], P('sfc'), may hold values from -0.5 to 0.5
- velocity: float32 [256, 3, 4096], P('sfc'), may hold values from -4 to 4
- neighbours: int32 [256, 6], P('sfc'), may hold values from -1 to 255, as said below
- refinement: int32 [512, 4], P('sfc'), may hold values from -1 to 255, as said below
Outputs:
- planes: float32 [256, 4, 4096], P('sfc')
- reflux: float32 [256, 6, 2, 256], P('sfc')
Inputs may be any that keep to these rules, and one draw needn't show every extreme that they name: `neighbours`: -1 marks the domain boundary; any other entry is a block on a device at most 2 away along the curve. `refinement`: each row is fine block, direction 0 to 5, coarse block, quadrant 0 to 3. A fine block of -1 marks an empty slot and a device's live slots come first; a live fine block is held by the device that holds the row; the coarse block lies on a device at most 2 away along the curve; every device has a live slot and some device has all 16 live.
All inputs are finite; a program needn't handle non-finite values.
Results may differ from a plain program's by a relative error of at most 0.0003.
Values sent between devices are 32-bit elements; how exact they have to be, the bound alone decides.
A program may use at most 64 MiB of HBM per device.

v0:
```python
import jax
import jax.numpy as jnp
from jax import lax
from jax.experimental import pallas as pl
from jax.experimental.pallas import tpu as pltpu
from jax.sharding import PartitionSpec as P

EDGE = 16
CELLS = 4096
REACH = 2
PASSES = 6
BLK = 8
NODES = (0.5 - 3.0**0.5 / 6.0, 0.5 + 3.0**0.5 / 6.0)
TIME_STEP = 0.25
DAMPING = 0.1
SHIFTS = (1, -1, 2, -2)
VEC = (8, 128)
ITEMS = 6
BLOCK_ROWS = ITEMS * 8
FINE_ROWS = 5 * 2 * 8
COARSE_ROWS = 5 * 2 * 2 * 16


def lanes():
    return lax.broadcasted_iota(jnp.int32, VEC, 1)


def take(values, index):
    return jnp.take_along_axis(values, index, axis=1, mode="promise_in_bounds")


def edge_index(swap):
    lane = lanes()
    kind = lane // 32
    if swap:
        kind = kind + 1 - 2 * (kind % 2)
    j = lane % 16
    source = jnp.where(
        kind == 0, j, jnp.where(kind == 1, 112 + j, (j % 8) * 16 + jnp.where(kind == 3, 15, 0))
    )
    upper = jnp.where(kind == 0, 0, jnp.where(kind == 1, 1, j // 8))
    return source, upper == 1, (lane // 16) % 2 == 1


def edges(tiles, index):
    source, upper, odd = index
    first = jnp.where(upper, take(tiles[1], source), take(tiles[0], source))
    second = jnp.where(upper, take(tiles[3], source), take(tiles[2], source))
    return jnp.where(odd, second, first)


def field_rows(fraction_ref, centroid_ref, field, start, size):
    if field == 0:
        return fraction_ref[:, pl.ds(start, size)]
    return centroid_ref[field - 1, :, pl.ds(start, size)]


def greet(count, me):
    barrier = pltpu.get_barrier_semaphore()
    for shift in SHIFTS:
        other = me + shift

        @pl.when((other >= 0) & (other < count))
        def _signal():
            pl.semaphore_signal(
                barrier, inc=1, device_id=(other,), device_id_type=pl.DeviceIdType.MESH
            )

    peers = sum(
        ((me + shift >= 0) & (me + shift < count)).astype(jnp.int32) for shift in SHIFTS
    )
    pl.semaphore_wait(barrier, peers)


def each_neighbour(count, me, action):
    for place, shift in enumerate(SHIFTS):
        other = me + shift

        @pl.when((other >= 0) & (other < count))
        def _act():
            action(place, shift, other)


def remote(src, dst, send, recv, other):
    return pltpu.make_async_remote_copy(
        src_ref=src,
        dst_ref=dst,
        send_sem=send,
        recv_sem=recv,
        device_id=(other,),
        device_id_type=pl.DeviceIdType.MESH,
    )


def faces_kernel(
    count, fraction_ref, centroid_ref, refine_ref, near_ref, table_ref, send, recv, send2, recv2
):
    me = lax.axis_index("sfc")
    near_own = REACH
    swapped = edge_index(True)
    plain = edge_index(False)

    def extract(slot, index, swap):
        for field in range(4):
            for pair in range(8):
                chunk = field_rows(fraction_ref, centroid_ref, field, pair * 512, 512)
                tiles = [chunk[:, 128 * t : 128 * t + 128] for t in range(4)]
                near_ref[slot, pl.ds(field * 8 + pair, 8, stride=BLOCK_ROWS), :] = edges(
                    tiles, index
                )
            for side in range(2):
                start = (1 - side if swap else side) * 3840
                for half in range(2):
                    near_ref[
                        slot, pl.ds(32 + half * 8 + side * 4 + field, 8, stride=BLOCK_ROWS), :
                    ] = field_rows(fraction_ref, centroid_ref, field, start + half * 128, 128)

    extract(near_own, swapped, True)
    table_ref[near_own] = refine_ref[...]
    greet(count, me)

    def start(place, shift, other):
        remote(
            near_ref.at[near_own], near_ref.at[REACH - shift], send.at[place], recv.at[place], other
        ).start()
        remote(
            refine_ref, table_ref.at[REACH - shift], send2.at[place], recv2.at[place], other
        ).start()

    each_neighbour(count, me, start)
    extract(2 * REACH + 1, plain, False)

    def finish_send(place, shift, other):
        remote(
            near_ref.at[near_own], near_ref.at[REACH - shift], send.at[place], recv.at[place], other
        ).wait_send()
        remote(
            refine_ref, table_ref.at[REACH - shift], send2.at[place], recv2.at[place], other
        ).wait_send()

    def finish_recv(place, shift, other):
        remote(
            near_ref.at[near_own], near_ref.at[REACH - shift], send.at[place], recv.at[place], other
        ).wait_recv()
        remote(
            refine_ref, table_ref.at[REACH - shift], send2.at[place], recv2.at[place], other
        ).wait_recv()

    each_neighbour(count, me, finish_send)
    for place, shift in enumerate(SHIFTS):
        other = me - shift

        @pl.when((other >= 0) & (other < count))
        def _recv():
            finish_recv(place, shift, other)


def packets_kernel(count, own_ref, near_ref, send, recv):
    me = lax.axis_index("sfc")
    greet(count, me)
    near_ref[REACH] = own_ref[...]

    def start(place, shift, other):
        remote(own_ref, near_ref.at[REACH - shift], send.at[place], recv.at[place], other).start()

    each_neighbour(count, me, start)

    def finish_send(place, shift, other):
        remote(
            own_ref, near_ref.at[REACH - shift], send.at[place], recv.at[place], other
        ).wait_send()

    each_neighbour(count, me, finish_send)
    for place, shift in enumerate(SHIFTS):
        other = me - shift

        @pl.when((other >= 0) & (other < count))
        def _recv():
            remote(
                own_ref, near_ref.at[REACH - shift], send.at[place], recv.at[place], other
            ).wait_recv()


def solve(h, g):
    (h00, h01, h02, h03, h11, h12, h13, h22, h23, h33) = h
    i0 = 1.0 / h00
    l10, l20, l30 = h01 * i0, h02 * i0, h03 * i0
    d1 = h11 - l10 * h01
    a21, a31 = h12 - l10 * h02, h13 - l10 * h03
    i1 = 1.0 / d1
    l21, l31 = a21 * i1, a31 * i1
    d2 = h22 - l20 * h02 - l21 * a21
    a32 = h23 - l20 * h03 - l21 * a31
    i2 = 1.0 / d2
    l32 = a32 * i2
    d3 = h33 - l30 * h03 - l31 * a31 - l32 * a32
    y1 = g[1] - l10 * g[0]
    y2 = g[2] - l20 * g[0] - l21 * y1
    y3 = g[3] - l30 * g[0] - l31 * y1 - l32 * y2
    x3 = y3 / d3
    x2 = y2 * i2 - l32 * x3
    x1 = y1 * i1 - l21 * x2 - l31 * x3
    x0 = g[0] * i0 - l10 * x1 - l20 * x2 - l30 * x3
    return x0, x1, x2, x3


def fit(points, params):
    def one_pass(_unused, params):
        a, b, c, d = params
        h = [None] * 10
        g = [None] * 4

        def add(total, place, term):
            total[place] = term if total[place] is None else total[place] + term

        for px, py, pz, f in points:
            t = jnp.tanh(a * px + b * py + c * pz + d)
            s = 1.0 - t * t
            q = s * s
            w = s * (t - f)
            qx, qy, qz = q * px, q * py, q * pz
            for place, term in enumerate(
                (qx * px, qx * py, qx * pz, qx, qy * py, qy * pz, qy, qz * pz, qz, q)
            ):
                add(h, place, term)
            for place, term in enumerate((w * px, w * py, w * pz, w)):
                add(g, place, term)
        for place in (0, 4, 7, 9):
            h[place] = h[place] + 4.0 * DAMPING
        step = solve(h, g)
        return tuple(p - s for p, s in zip(params, step))

    return lax.fori_loop(0, PASSES, one_pass, params)


def fit_kernel(
    fraction_ref,
    centroid_ref,
    velocity_ref,
    near_ref,
    neighbours_ref,
    refine_ref,
    planes_ref,
    comps_ref,
    packets_ref,
    padded,
    ghost_edges,
    ghost_layers,
    fine_table,
):
    me = lax.axis_index("sfc")
    lane = lanes()
    row = lax.broadcasted_iota(jnp.int32, VEC, 0)
    first_block = (me - REACH) * BLK

    for block in range(BLK):
        place = []
        for k in range(6):
            other = neighbours_ref[block, k]
            place.append(
                jnp.where(
                    other >= 0,
                    jnp.clip(other - first_block, 0, (2 * REACH + 1) * BLK - 1),
                    (2 * REACH + 1) * BLK + block,
                )
            )
        for field in range(4):
            value = near_ref[place[5], field]
            for k in (4, 3, 2):
                value = jnp.where(lane < (k - 1) * 32, near_ref[place[k], field], value)
            ghost_edges[block * 32 + field * 8 : block * 32 + field * 8 + 8, :] = value
        for half in range(2):
            ghost_layers[half, block * 8 : block * 8 + 8, :] = jnp.where(
                row < 4, near_ref[place[0], 4 + half], near_ref[place[1], 4 + half]
            )

    for field in range(4):
        for half in range(2):
            for side in range(2):
                start = side * 4352 + half * 128
                padded[field, :, start : start + 128] = ghost_layers[
                    half, pl.ds(side * 4 + field, 8, stride=8), :
                ]
        padded[field, :, 256:4352] = field_rows(fraction_ref, centroid_ref, field, 0, CELLS)

    wide = lax.broadcasted_iota(jnp.int32, (8, 512), 1)
    y_pos = wide // 16 % 16
    z_pos = wide % 16
    plain = edge_index(False)
    y_source, z_source = [], []
    for tile in range(4):
        odd, upper = tile // 2, tile % 2
        y_source.append(upper * 32 + odd * 16 + lane % 16)
        z_source.append(
            jnp.where(lane % 16 < 8, 64, 96) + odd * 16 + upper * 8 + lane // 16
        )

    def one_pair(pair, carry):
        start = pl.multiple_of(pair * 512, 512)
        fields = [[] for _unused in range(7)]
        for field in range(4):
            center = padded[field, :, pl.ds(start + 256, 512)]
            ghost = ghost_edges[pl.ds(field * 8 + pair, 8, stride=32), :]
            ghost_y = jnp.concatenate([take(ghost, i) for i in y_source], 1)
            ghost_z = jnp.concatenate([take(ghost, i) for i in z_source], 1)
            fields[0].append(center)
            fields[1].append(padded[field, :, pl.ds(start, 512)])
            fields[2].append(padded[field, :, pl.ds(start + 512, 512)])
            fields[3].append(jnp.where(y_pos == 0, ghost_y, pltpu.roll(center, 16, 1)))
            fields[4].append(jnp.where(y_pos == 15, ghost_y, pltpu.roll(center, 496, 1)))
            fields[5].append(jnp.where(z_pos == 0, ghost_z, pltpu.roll(center, 1, 1)))
            fields[6].append(jnp.where(z_pos == 15, ghost_z, pltpu.roll(center, 511, 1)))
        a, b, c = [2.0 * (fields[2 + 2 * i][0] - fields[1 + 2 * i][0]) for i in range(3)]
        frac, cx, cy, cz = fields[0]
        d = 2.0 * (2.0 * frac - 1.0) - a * cx - b * cy - c * cz
        points = [(cx, cy, cz, 2.0 * frac - 1.0)]
        for k in range(6):
            f, *coords = fields[k + 1]
            coords[k // 2] = coords[k // 2] + (2.0 * (k % 2) - 1.0)
            points.append((*coords, 2.0 * f - 1.0))
        params = fit(points, (a, b, c, d))
        for comp in range(4):
            planes_ref[:, comp, pl.ds(start, 512)] = params[comp]
            comps_ref[comp, :, pl.ds(start, 512)] = params[comp]
            tiles = [params[comp][:, 128 * t : 128 * t + 128] for t in range(4)]
            fine_table[pl.ds(comp * 16 + 8 + pair, 8, stride=FINE_ROWS), :] = edges(tiles, plain)
        speeds = []
        for axis in (1, 2):
            chunk = velocity_ref[axis, :, pl.ds(start, 512)]
            speeds.append(edges([chunk[:, 128 * t : 128 * t + 128] for t in range(4)], plain))
        fine_table[pl.ds(4 * 16 + 8 + pair, 8, stride=FINE_ROWS), :] = jnp.where(
            lane < 64, speeds[0], speeds[1]
        )
        return carry

    lax.fori_loop(0, 8, one_pair, 0)

    for comp in range(5):
        for half in range(2):
            sides = []
            for side in range(2):
                start = side * 3840 + half * 128
                if comp < 4:
                    sides.append(comps_ref[comp, :, start : start + 128])
                else:
                    sides.append(velocity_ref[0, :, start : start + 128])
            for part in range(4):
                low = sides[0] if part == 0 else pltpu.roll(sides[0], 128 - 32 * part, 1)
                high = sides[1] if part == 1 else pltpu.roll(sides[1], (160 - 32 * part) % 128, 1)
                fine_table[pl.ds(comp * 16 + half * 4 + part, 8, stride=FINE_ROWS), :] = jnp.where(
                    lane < 32, low, high
                )

    for slot in range(refine_ref.shape[0]):
        block = jnp.clip(refine_ref[slot, 0] - me * BLK, 0, BLK - 1)
        k = jnp.clip(refine_ref[slot, 1], 0, 5)
        yz = (k >= 2).astype(jnp.int32)
        base = block * FINE_ROWS + yz * 8
        group = k - 2 * yz
        parts = []
        for target, comp in enumerate((k // 2, 3, 4)):
            value = fine_table[pl.ds(pl.multiple_of(base + comp * 16, 8), 8), :]
            parts.append(pltpu.roll(value, (128 + 32 * target - 32 * group) % 128, 1))
        packets_ref[slot] = jnp.where(
            lane < 32, parts[0], jnp.where(lane < 64, parts[1], parts[2])
        )


def flux_kernel(
    comps_ref, velocity_ref, packets_ref, table_ref, reflux_ref, coarse_table, sums, live_list
):
    me = lax.axis_index("sfc")
    lane = lanes()
    kind = lane // 32
    pos = lane % 32
    cell = pos % 16 // 2
    slots = packets_ref.shape[1]
    total = packets_ref.shape[0] * slots

    def collect(item, found):
        offset = item // slots
        slot = item % slots
        coarse = table_ref[offset, slot, 2]
        other = me + offset - REACH
        there = (other >= 0) & (other < lax.axis_size("sfc"))
        mine = there & (table_ref[offset, slot, 0] >= 0) & (coarse >= 0) & (coarse // BLK == me)

        @pl.when(mine)
        def _keep():
            live_list[found] = item

        return found + mine.astype(jnp.int32)

    found = lax.fori_loop(0, total, collect, 0)
    for extra in range(3):
        live_list[found + extra] = REACH * slots

    sums[...] = jnp.zeros_like(sums)

    def build(x, carry):
        start = pl.multiple_of(x * 256, 256)
        x_tile = pl.multiple_of(x // 8 * 128, 128)
        for qb in range(2):
            source = jnp.where(
                kind == 0,
                qb * 8 + cell,
                jnp.where(kind == 1, 112 + qb * 8 + cell, cell * 16 + jnp.where(kind == 3, 15, 0)),
            )
            upper = jnp.where(kind == 0, 0, jnp.where(kind == 1, 1, qb)) == 1
            layer_source = x % 8 * 16 + qb * 8 + cell
            for comp in range(5):
                if comp < 4:
                    value = jnp.where(
                        upper,
                        take(comps_ref[comp, :, pl.ds(start + 128, 128)], source),
                        take(comps_ref[comp, :, pl.ds(start, 128)], source),
                    )
                    low = comps_ref[comp, :, pl.ds(x_tile, 128)]
                    high = comps_ref[comp, :, pl.ds(x_tile + 3840, 128)]
                else:
                    by_axis = [
                        jnp.where(
                            upper,
                            take(velocity_ref[axis, :, pl.ds(start + 128, 128)], source),
                            take(velocity_ref[axis, :, pl.ds(start, 128)], source),
                        )
                        for axis in (1, 2)
                    ]
                    value = jnp.where(lane < 64, by_axis[0], by_axis[1])
                    low = velocity_ref[0, :, pl.ds(x_tile, 128)]
                    high = velocity_ref[0, :, pl.ds(x_tile + 3840, 128)]
                layer = jnp.where(lane < 32, take(low, layer_source), take(high, layer_source))
                base = comp * 64 + qb * 16
                coarse_table[pl.ds(base + x, 8, stride=COARSE_ROWS), :] = layer
                coarse_table[pl.ds(base + 32 + x, 8, stride=COARSE_ROWS), :] = value
        return carry

    lax.fori_loop(0, 16, build, 0)

    offset_one = ((pos // 16).astype(jnp.float32) - 0.5) * 0.5
    offset_two = ((pos % 2).astype(jnp.float32) - 0.5) * 0.5

    def moments(item, weight):
        offset = item // slots
        slot = item % slots
        k = jnp.clip(table_ref[offset, slot, 1], 0, 5)
        block = jnp.clip(table_ref[offset, slot, 2] - me * BLK, 0, BLK - 1)
        quadrant = jnp.clip(table_ref[offset, slot, 3], 0, 3)
        qa, qb = quadrant // 2, quadrant % 2
        facing = k + 1 - 2 * (k % 2)
        axis = k // 2
        sign = (2 * (k % 2) - 1).astype(jnp.float32)
        yz = (k >= 2).astype(jnp.int32)
        shift = (128 - 32 * (facing - 2 * yz)) % 128
        base = block * COARSE_ROWS + yz * 32 + qb * 16 + qa * 8
        first = jnp.where(axis == 0, 1, 0)
        second = jnp.where(axis == 2, 1, 2)
        normal_c, one_c, two_c, d_c, u_c = [
            pltpu.roll(
                coarse_table[pl.ds(pl.multiple_of(base + comp * 64, 8), 8), :], shift, 1
            )
            for comp in (axis, first, second, 3, 4)
        ]
        packet = packets_ref[offset, slot]
        normal_f = packet
        d_f = pltpu.roll(packet, 96, 1)
        u_f = pltpu.roll(packet, 64, 1)
        speed = sign * 0.5 * (u_f + u_c)
        depth = jnp.abs(speed) * TIME_STEP
        outflow = jnp.maximum(speed, 0.0)
        inflow = jnp.minimum(speed, 0.0)
        tangent = one_c * offset_one + two_c * offset_two + d_c
        volume = jnp.zeros(VEC, jnp.float32)
        moment = jnp.zeros(VEC, jnp.float32)
        for node in NODES:
            fine_model = 0.5 * (
                1.0 + jnp.tanh(normal_f * (sign * (0.5 - node * depth)) + d_f)
            )
            coarse_model = 0.5 * (
                1.0 + jnp.tanh(normal_c * (-sign * (0.5 - 0.5 * node * depth)) + tangent)
            )
            volume = volume + 0.5 * TIME_STEP * (outflow * fine_model + inflow * coarse_model)
            moment = moment + 0.5 * TIME_STEP * node * depth * sign * (
                inflow * coarse_model - outflow * fine_model
            )
        both = jnp.where(
            lane < 32, volume, jnp.where((lane >= 64) & (lane < 96), pltpu.roll(moment, 64, 1), 0.0)
        )
        both = jnp.where(weight, both, 0.0)
        target = pl.multiple_of((block * 6 + facing) * 16 + qa * 8, 8)
        return pltpu.roll(both, 32 * qb, 1), target

    def group(number, carry):
        results = [
            moments(live_list[number * 4 + i], number * 4 + i < found) for i in range(4)
        ]
        for value, target in results:
            sums[pl.ds(target, 8), :] += value
        return carry

    lax.fori_loop(0, (found + 3) // 4, group, 0)

    j = lane % 16
    for tile in range(6):
        outs = [[jnp.zeros(VEC, jnp.float32)] * 2 for _unused in range(2)]
        for i in range(16):
            value = sums[pl.ds(tile * 128 + i, 8, stride=16), :]
            value = value + pltpu.roll(value, 127, 1)
            value = value + pltpu.roll(value, 112, 1)
            for m in range(2):
                placed = take(value, m * 64 + j // 8 * 32 + 2 * (j % 8))
                outs[m][i // 8] = jnp.where(lane // 16 == i % 8, placed, outs[m][i // 8])
        for m in range(2):
            for half in range(2):
                start = m * 256 + half * 128
                reflux_ref[tile * 8 : tile * 8 + 8, start : start + 128] = outs[m][half]


def spec(space):
    return pl.BlockSpec(memory_space=space)


def per_device(fraction, centroid, velocity, neighbours, refinement):
    count = lax.axis_size("sfc")
    slots = refinement.shape[0]
    vmem, smem = spec(pltpu.VMEM), spec(pltpu.SMEM)
    f32 = jnp.float32
    centroid, velocity = jnp.swapaxes(centroid, 0, 1), jnp.swapaxes(velocity, 0, 1)
    near, table = pl.pallas_call(
        lambda *refs: faces_kernel(count, *refs),
        out_shape=(
            jax.ShapeDtypeStruct((6, BLK * BLOCK_ROWS, 128), f32),
            jax.ShapeDtypeStruct((5, slots, 4), jnp.int32),
        ),
        in_specs=[vmem] * 3,
        out_specs=(vmem, vmem),
        scratch_shapes=[pltpu.SemaphoreType.DMA((4,))] * 4,
        compiler_params=pltpu.CompilerParams(collective_id=0, has_side_effects=True),
        name="exchange_faces",
    )(fraction, centroid, refinement)
    planes, comps, packets = pl.pallas_call(
        fit_kernel,
        out_shape=(
            jax.ShapeDtypeStruct((BLK, 4, CELLS), f32),
            jax.ShapeDtypeStruct((4, BLK, CELLS), f32),
            jax.ShapeDtypeStruct((slots, 8, 128), f32),
        ),
        in_specs=[vmem] * 4 + [smem] * 2,
        out_specs=(vmem,) * 3,
        scratch_shapes=[
            pltpu.VMEM((4, 8, CELLS + 512), f32),
            pltpu.VMEM((256, 128), f32),
            pltpu.VMEM((2, 64, 128), f32),
            pltpu.VMEM((BLK * FINE_ROWS, 128), f32),
        ],
        name="fit_planes",
    )(fraction, centroid, velocity, near.reshape(48, ITEMS, 8, 128), neighbours, refinement)
    near_packets = pl.pallas_call(
        lambda *refs: packets_kernel(count, *refs),
        out_shape=jax.ShapeDtypeStruct((5, slots, 8, 128), f32),
        in_specs=[vmem],
        out_specs=vmem,
        scratch_shapes=[pltpu.SemaphoreType.DMA((4,))] * 2,
        compiler_params=pltpu.CompilerParams(collective_id=1, has_side_effects=True),
        name="exchange_packets",
    )(packets)
    reflux = pl.pallas_call(
        flux_kernel,
        out_shape=jax.ShapeDtypeStruct((BLK * 6, 512), f32),
        in_specs=[vmem] * 3 + [smem],
        out_specs=vmem,
        scratch_shapes=[
            pltpu.VMEM((BLK * COARSE_ROWS, 128), f32),
            pltpu.VMEM((BLK * 6 * 16, 128), f32),
            pltpu.SMEM((5 * slots + 4,), jnp.int32),
        ],
        name="reflux_moments",
    )(comps, velocity, near_packets, table)
    return planes, reflux.reshape(BLK, 6, 2, 256)


def solution(mesh):
    return jax.shard_map(
        per_device,
        mesh=mesh,
        in_specs=(
            P("sfc", None),
            P("sfc", None, None),
            P("sfc", None, None),
            P("sfc", None),
            P("sfc", None),
        ),
        out_specs=(P("sfc", None, None), P("sfc", None, None, None)),
        check_vma=False,
    )
```

profile of v0, /device:TPU:0, one launch (start us, length us, event | category | flops | bytes accessed | tf_op | source)
XLA Modules:
  0.0 65.3 jit_solution(3560178967412889872)
XLA Ops:
  0.6 1.4 %copy.7.refs_2_.refine_ref = s32[16,4]{1,0:T(8,128)} copy(s32[16,4]{0,1:T(4,128)} %param.9) | data formatting | bytes 512 | tf_op args[4]
  2.0 21.0 %exchange_faces.1 = (f32[6,384,128]{2,1,0:T(8,128)}, s32[5,16,4]{2,1,0:T(8,128)}) custom-call(f32[8,4096]{1,0:T(8,128)} %fraction_ref.1, f32[3,8,4096]{2,1,0:T(8,128)} %bitcast.3, s32[16,4]{1,0:T(8,128)} %copy.7.refs_2_.refine_ref), custom_call_target="tpu_custom_call" | custom-call | tf_op jit(solution)/shard_map/exchange_faces/pallas_call | solution.py:529
  23.0 15.9 %fit_planes.1 = (f32[8,4,4096]{2,1,0:T(4,128)}, f32[4,8,4096]{2,1,0:T(8,128)}, f32[16,8,128]{2,1,0:T(8,128)}) custom-call(f32[8,4096]{1,0:T(8,128)} %fraction_ref.1, f32[3,8,4096]{2,1,0:T(8,128)} %bitcast.4, f32[3,8,4096]{2,1,0:T(8,128)} %bitcast.5, f32[48,6,8,128]{3,2,1,0:T(8,128)} %bitcast.7, s32[8,6]{1,0:T(8,128)} %neighbours_ref.1, ...), custom_call_target="tpu_custom_call" | custom-call | tf_op jit(solution)/shard_map/fit_planes/pallas_call | solution.py:541
  38.9 8.7 %exchange_packets.1.packets_ref = f32[5,16,8,128]{3,2,1,0:T(8,128)} custom-call(f32[16,8,128]{2,1,0:T(8,128)} %get-tuple-element.10.refs_0_), custom_call_target="tpu_custom_call" | custom-call | tf_op jit(solution)/shard_map/exchange_packets/pallas_call | solution.py:558
  47.6 16.1 %reflux_moments.1 = f32[48,512]{1,0:T(8,128)} custom-call(f32[4,8,4096]{2,1,0:T(8,128)} %get-tuple-element.9.comps_ref, f32[3,8,4096]{2,1,0:T(8,128)} %bitcast.6, f32[5,16,8,128]{3,2,1,0:T(8,128)} %exchange_packets.1.packets_ref, s32[5,16,4]{2,1,0:T(8,128)} %get-tuple-element.11.table_ref), custom_call_target="tpu_custom_call" | custom-call | tf_op jit(solution)/shard_map/reflux_moments/pallas_call | solution.py:567
  63.7 1.6 %reshape.11 = f32[8,6,2,256]{3,2,1,0:T(2,128)} reshape(f32[48,512]{1,0:T(8,128)} %reflux_moments.1) | data formatting | bytes 196608 | tf_op jit(solution)/shard_map/reshape | solution.py:579
where the time goes:
time: 65.4 us; the launch traced here: 65.3 us
  Pallas kernels  61.7 us (94%)
  local copies, waits for them, and re-layouts  2.95 us (5%)
    pallas_call x1, Pallas kernels, per_device(): pl.pallas_call(lambda *refs: faces_kernel(count, *refs), out_shape=(jax.S...  21 us
    pallas_call x1, Pallas kernels, per_device(): pl.pallas_call(flux_kernel, out_shape=jax.ShapeDtypeStruct((BLK * 6, 512)...  16.1 us
    pallas_call x1, Pallas kernels, per_device(): pl.pallas_call(fit_kernel, out_shape=(jax.ShapeDtypeStruct((BLK, 4, CELLS...  15.9 us
    pallas_call x1, Pallas kernels, per_device(): pl.pallas_call(lambda *refs: packets_kernel(count, *refs), out_shape=jax....  8.69 us
    reshape x1, local copies, waits for them, and re-layouts, per_device(): return (planes, reflux.reshape(BLK, 6, 2, 256))  1.59 us
    unnamed x1, local copies, waits for them, and re-layouts  1.35 us

commit v1 on v0

--- a/solution.py
+++ b/solution.py
@@ -18,7 +18,6 @@
 ITEMS = 6
 BLOCK_ROWS = ITEMS * 8
 FINE_ROWS = 5 * 2 * 8
-COARSE_ROWS = 5 * 2 * 2 * 16
 
 
 def lanes():
@@ -241,12 +240,11 @@
     neighbours_ref,
     refine_ref,
     planes_ref,
-    comps_ref,
+    fine_table,
     packets_ref,
     padded,
     ghost_edges,
     ghost_layers,
-    fine_table,
 ):
     me = lax.axis_index("sfc")
     lane = lanes()
@@ -321,7 +319,6 @@
         params = fit(points, (a, b, c, d))
         for comp in range(4):
             planes_ref[:, comp, pl.ds(start, 512)] = params[comp]
-            comps_ref[comp, :, pl.ds(start, 512)] = params[comp]
             tiles = [params[comp][:, 128 * t : 128 * t + 128] for t in range(4)]
             fine_table[pl.ds(comp * 16 + 8 + pair, 8, stride=FINE_ROWS), :] = edges(tiles, plain)
         speeds = []
@@ -341,7 +338,7 @@
             for side in range(2):
                 start = side * 3840 + half * 128
                 if comp < 4:
-                    sides.append(comps_ref[comp, :, start : start + 128])
+                    sides.append(planes_ref[:, comp, start : start + 128])
                 else:
                     sides.append(velocity_ref[0, :, start : start + 128])
             for part in range(4):
@@ -351,9 +348,9 @@
                     lane < 32, low, high
                 )
 
-    for slot in range(refine_ref.shape[0]):
-        block = jnp.clip(refine_ref[slot, 0] - me * BLK, 0, BLK - 1)
-        k = jnp.clip(refine_ref[slot, 1], 0, 5)
+    for slot in range(refine_ref.shape[1]):
+        block = jnp.clip(refine_ref[0, slot] - me * BLK, 0, BLK - 1)
+        k = jnp.clip(refine_ref[1, slot], 0, 5)
         yz = (k >= 2).astype(jnp.int32)
         base = block * FINE_ROWS + yz * 8
         group = k - 2 * yz
@@ -366,76 +363,30 @@
         )
 
 
-def flux_kernel(
-    comps_ref, velocity_ref, packets_ref, table_ref, reflux_ref, coarse_table, sums, live_list
-):
+def flux_kernel(faces_ref, packets_ref, table_ref, reflux_ref, live_list):
     me = lax.axis_index("sfc")
     lane = lanes()
-    kind = lane // 32
+    row = lax.broadcasted_iota(jnp.int32, VEC, 0)
     pos = lane % 32
     cell = pos % 16 // 2
     slots = packets_ref.shape[1]
-    total = packets_ref.shape[0] * slots
-
-    def collect(item, found):
-        offset = item // slots
-        slot = item % slots
-        coarse = table_ref[offset, slot, 2]
+
+    found = 0
+    for offset in range(2 * REACH + 1):
         other = me + offset - REACH
         there = (other >= 0) & (other < lax.axis_size("sfc"))
-        mine = there & (table_ref[offset, slot, 0] >= 0) & (coarse >= 0) & (coarse // BLK == me)
-
-        @pl.when(mine)
-        def _keep():
-            live_list[found] = item
-
-        return found + mine.astype(jnp.int32)
-
-    found = lax.fori_loop(0, total, collect, 0)
+
+        def collect(slot, found):
+            local = table_ref[offset, 2, slot] - me * BLK
+            mine = there & (table_ref[offset, 0, slot] >= 0) & (local >= 0) & (local < BLK)
+            live_list[found] = offset * slots + slot
+            return found + mine.astype(jnp.int32)
+
+        found = lax.fori_loop(0, slots, collect, found, unroll=4 if slots % 4 == 0 else 1)
     for extra in range(3):
         live_list[found + extra] = REACH * slots
 
-    sums[...] = jnp.zeros_like(sums)
-
-    def build(x, carry):
-        start = pl.multiple_of(x * 256, 256)
-        x_tile = pl.multiple_of(x // 8 * 128, 128)
-        for qb in range(2):
-            source = jnp.where(
-                kind == 0,
-                qb * 8 + cell,
-                jnp.where(kind == 1, 112 + qb * 8 + cell, cell * 16 + jnp.where(kind == 3, 15, 0)),
-            )
-            upper = jnp.where(kind == 0, 0, jnp.where(kind == 1, 1, qb)) == 1
-            layer_source = x % 8 * 16 + qb * 8 + cell
-            for comp in range(5):
-                if comp < 4:
-                    value = jnp.where(
-                        upper,
-                        take(comps_ref[comp, :, pl.ds(start + 128, 128)], source),
-                        take(comps_ref[comp, :, pl.ds(start, 128)], source),
-                    )
-                    low = comps_ref[comp, :, pl.ds(x_tile, 128)]
-                    high = comps_ref[comp, :, pl.ds(x_tile + 3840, 128)]
-                else:
-                    by_axis = [
-                        jnp.where(
-                            upper,
-                            take(velocity_ref[axis, :, pl.ds(start + 128, 128)], source),
-                            take(velocity_ref[axis, :, pl.ds(start, 128)], source),
-                        )
-                        for axis in (1, 2)
-                    ]
-                    value = jnp.where(lane < 64, by_axis[0], by_axis[1])
-                    low = velocity_ref[0, :, pl.ds(x_tile, 128)]
-                    high = velocity_ref[0, :, pl.ds(x_tile + 3840, 128)]
-                layer = jnp.where(lane < 32, take(low, layer_source), take(high, layer_source))
-                base = comp * 64 + qb * 16
-                coarse_table[pl.ds(base + x, 8, stride=COARSE_ROWS), :] = layer
-                coarse_table[pl.ds(base + 32 + x, 8, stride=COARSE_ROWS), :] = value
-        return carry
-
-    lax.fori_loop(0, 16, build, 0)
+    reflux_ref[...] = jnp.zeros_like(reflux_ref)
 
     offset_one = ((pos // 16).astype(jnp.float32) - 0.5) * 0.5
     offset_two = ((pos % 2).astype(jnp.float32) - 0.5) * 0.5
@@ -443,21 +394,28 @@
     def moments(item, weight):
         offset = item // slots
         slot = item % slots
-        k = jnp.clip(table_ref[offset, slot, 1], 0, 5)
-        block = jnp.clip(table_ref[offset, slot, 2] - me * BLK, 0, BLK - 1)
-        quadrant = jnp.clip(table_ref[offset, slot, 3], 0, 3)
+        k = jnp.clip(table_ref[offset, 1, slot], 0, 5)
+        block = jnp.clip(table_ref[offset, 2, slot] - me * BLK, 0, BLK - 1)
+        quadrant = jnp.clip(table_ref[offset, 3, slot], 0, 3)
         qa, qb = quadrant // 2, quadrant % 2
         facing = k + 1 - 2 * (k % 2)
         axis = k // 2
         sign = (2 * (k % 2) - 1).astype(jnp.float32)
         yz = (k >= 2).astype(jnp.int32)
-        shift = (128 - 32 * (facing - 2 * yz)) % 128
-        base = block * COARSE_ROWS + yz * 32 + qb * 16 + qa * 8
+        from_row = qa * 4 + row // 2
+        from_lane = (facing - 2 * yz) * 32 + row % 2 * 16 + qb * 8 + cell
+        base = block * FINE_ROWS + yz * 8
         first = jnp.where(axis == 0, 1, 0)
         second = jnp.where(axis == 2, 1, 2)
         normal_c, one_c, two_c, d_c, u_c = [
-            pltpu.roll(
-                coarse_table[pl.ds(pl.multiple_of(base + comp * 64, 8), 8), :], shift, 1
+            take(
+                jnp.take_along_axis(
+                    faces_ref[pl.ds(pl.multiple_of(base + comp * 16, 8), 8), :],
+                    from_row,
+                    axis=0,
+                    mode="promise_in_bounds",
+                ),
+                from_lane,
             )
             for comp in (axis, first, second, 3, 4)
         ]
@@ -483,37 +441,27 @@
             moment = moment + 0.5 * TIME_STEP * node * depth * sign * (
                 inflow * coarse_model - outflow * fine_model
             )
-        both = jnp.where(
-            lane < 32, volume, jnp.where((lane >= 64) & (lane < 96), pltpu.roll(moment, 64, 1), 0.0)
-        )
-        both = jnp.where(weight, both, 0.0)
-        target = pl.multiple_of((block * 6 + facing) * 16 + qa * 8, 8)
-        return pltpu.roll(both, 32 * qb, 1), target
+        both = jnp.where(lane < 32, volume, pltpu.roll(moment, 32, 1))
+        both = both + pltpu.roll(both, 127, 1)
+        both = both + pltpu.roll(both, 112, 1)
+        keep = (lane // 16 == row) & (lane % 16 // 8 == qb) & weight
+        rows = []
+        for m in range(2):
+            placed = jnp.where(keep, take(both, m * 32 + 2 * (lane % 8)), 0.0)
+            rows.append(jnp.sum(placed, axis=0, keepdims=True))
+        return rows, block, facing, qa
 
     def group(number, carry):
         results = [
             moments(live_list[number * 4 + i], number * 4 + i < found) for i in range(4)
         ]
-        for value, target in results:
-            sums[pl.ds(target, 8), :] += value
+        for rows, block, facing, qa in results:
+            start = pl.multiple_of(qa * 128, 128)
+            for m in range(2):
+                reflux_ref[block, facing, m : m + 1, pl.ds(start, 128)] += rows[m]
         return carry
 
     lax.fori_loop(0, (found + 3) // 4, group, 0)
-
-    j = lane % 16
-    for tile in range(6):
-        outs = [[jnp.zeros(VEC, jnp.float32)] * 2 for _unused in range(2)]
-        for i in range(16):
-            value = sums[pl.ds(tile * 128 + i, 8, stride=16), :]
-            value = value + pltpu.roll(value, 127, 1)
-            value = value + pltpu.roll(value, 112, 1)
-            for m in range(2):
-                placed = take(value, m * 64 + j // 8 * 32 + 2 * (j % 8))
-                outs[m][i // 8] = jnp.where(lane // 16 == i % 8, placed, outs[m][i // 8])
-        for m in range(2):
-            for half in range(2):
-                start = m * 256 + half * 128
-                reflux_ref[tile * 8 : tile * 8 + 8, start : start + 128] = outs[m][half]
 
 
 def spec(space):
@@ -525,12 +473,13 @@
     slots = refinement.shape[0]
     vmem, smem = spec(pltpu.VMEM), spec(pltpu.SMEM)
     f32 = jnp.float32
+    refinement = refinement.T
     centroid, velocity = jnp.swapaxes(centroid, 0, 1), jnp.swapaxes(velocity, 0, 1)
     near, table = pl.pallas_call(
         lambda *refs: faces_kernel(count, *refs),
         out_shape=(
             jax.ShapeDtypeStruct((6, BLK * BLOCK_ROWS, 128), f32),
-            jax.ShapeDtypeStruct((5, slots, 4), jnp.int32),
+            jax.ShapeDtypeStruct((5, 4, slots), jnp.int32),
         ),
         in_specs=[vmem] * 3,
         out_specs=(vmem, vmem),
@@ -538,11 +487,11 @@
         compiler_params=pltpu.CompilerParams(collective_id=0, has_side_effects=True),
         name="exchange_faces",
     )(fraction, centroid, refinement)
-    planes, comps, packets = pl.pallas_call(
+    planes, faces, packets = pl.pallas_call(
         fit_kernel,
         out_shape=(
             jax.ShapeDtypeStruct((BLK, 4, CELLS), f32),
-            jax.ShapeDtypeStruct((4, BLK, CELLS), f32),
+            jax.ShapeDtypeStruct((BLK * FINE_ROWS, 128), f32),
             jax.ShapeDtypeStruct((slots, 8, 128), f32),
         ),
         in_specs=[vmem] * 4 + [smem] * 2,
@@ -551,7 +500,6 @@
             pltpu.VMEM((4, 8, CELLS + 512), f32),
             pltpu.VMEM((256, 128), f32),
             pltpu.VMEM((2, 64, 128), f32),
-            pltpu.VMEM((BLK * FINE_ROWS, 128), f32),
         ],
         name="fit_planes",
     )(fraction, centroid, velocity, near.reshape(48, ITEMS, 8, 128), neighbours, refinement)
@@ -566,17 +514,13 @@
     )(packets)
     reflux = pl.pallas_call(
         flux_kernel,
-        out_shape=jax.ShapeDtypeStruct((BLK * 6, 512), f32),
-        in_specs=[vmem] * 3 + [smem],
+        out_shape=jax.ShapeDtypeStruct((BLK, 6, 2, 256), f32),
+        in_specs=[vmem] * 2 + [smem],
         out_specs=vmem,
-        scratch_shapes=[
-            pltpu.VMEM((BLK * COARSE_ROWS, 128), f32),
-            pltpu.VMEM((BLK * 6 * 16, 128), f32),
-            pltpu.SMEM((5 * slots + 4,), jnp.int32),
-        ],
+        scratch_shapes=[pltpu.SMEM((5 * slots + 4,), jnp.int32)],
         name="reflux_moments",
-    )(comps, velocity, near_packets, table)
-    return planes, reflux.reshape(BLK, 6, 2, 256)
+    )(faces, near_packets, table)
+    return planes, reflux
 
 
 def solution(mesh):

time: 65.4 us -> 50.1 us (0.77); the launches traced: 65.3 us -> 49.2 us
  Pallas kernels: 61.7 us -> 48.6 us
  local copies, waits for them, and re-layouts: 2.95 us -> 0 us
    pallas_call x1, Pallas kernels: 16.1 us -> 3.42 us  [per_device(): pl.pallas_call(flux_kernel, out_shape=jax.ShapeDtypeStruct((BLK, 6, 2, 25...]
    reshape x1 -> x0, local copies, waits for them, and re-layouts: 1.59 us -> none  [per_device(): return (planes, reflux.reshape(BLK, 6, 2, 256))]
    unnamed x1 -> x0, local copies, waits for them, and re-layouts: 1.35 us -> none
where the time goes in v1:
time: 50.1 us; the launch traced here: 49.2 us
  Pallas kernels  48.6 us (97%)
  between operations  0.65 us (1%)
    pallas_call x1, Pallas kernels, per_device(): pl.pallas_call(lambda *refs: faces_kernel(count, *refs), out_shape=(jax.S...  20.6 us
    pallas_call x1, Pallas kernels, per_device(): pl.pallas_call(fit_kernel, out_shape=(jax.ShapeDtypeStruct((BLK, 4, CELLS...  15.9 us
    pallas_call x1, Pallas kernels, per_device(): pl.pallas_call(lambda *refs: packets_kernel(count, *refs), out_shape=jax....  8.69 us
    pallas_call x1, Pallas kernels, per_device(): pl.pallas_call(flux_kernel, out_shape=jax.ShapeDtypeStruct((BLK, 6, 2, 25...  3.42 us

profile of v1, /device:TPU:0, one launch (start us, length us, event | category | flops | bytes accessed | tf_op | source)
XLA Modules:
  0.0 49.2 jit_solution(4810896395484269882)
XLA Ops:
  0.6 20.6 %exchange_faces.1 = (f32[6,384,128]{2,1,0:T(8,128)}, s32[5,4,16]{2,1,0:T(4,128)}) custom-call(f32[8,4096]{1,0:T(8,128)} %fraction_ref.1, f32[3,8,4096]{2,1,0:T(8,128)} %bitcast.4, s32[4,16]{1,0:T(4,128)} %bitcast.8), custom_call_target="tpu_custom_call" | custom-call | tf_op jit(solution)/shard_map/exchange_faces/pallas_call | solution.py:478
  21.2 15.9 %fit_planes.1 = (f32[8,4,4096]{2,1,0:T(4,128)}, f32[640,128]{1,0:T(8,128)}, f32[16,8,128]{2,1,0:T(8,128)}) custom-call(f32[8,4096]{1,0:T(8,128)} %fraction_ref.1, f32[3,8,4096]{2,1,0:T(8,128)} %bitcast.5, f32[3,8,4096]{2,1,0:T(8,128)} %bitcast.7, f32[48,6,8,128]{3,2,1,0:T(8,128)} %bitcast.6, s32[8,6]{1,0:T(8,128)} %neighbours_ref.1, s32[4,16]{1,0:T(4,128)} %bitcast.9), custom_call_target="tpu_custom_call" | custom-call | tf_op jit(solution)/shard_map/fit_planes/pallas_call | solution.py:490
  37.1 8.7 %exchange_packets.1.packets_ref = f32[5,16,8,128]{3,2,1,0:T(8,128)} custom-call(f32[16,8,128]{2,1,0:T(8,128)} %get-tuple-element.10.refs_0_), custom_call_target="tpu_custom_call" | custom-call | tf_op jit(solution)/shard_map/exchange_packets/pallas_call | solution.py:506
  45.8 3.4 %reflux_moments.1 = f32[8,6,2,256]{3,2,1,0:T(2,128)} custom-call(f32[640,128]{1,0:T(8,128)} %get-tuple-element.9.faces_ref, f32[5,16,8,128]{3,2,1,0:T(8,128)} %exchange_packets.1.packets_ref, s32[5,4,16]{2,1,0:T(4,128)} %get-tuple-element.11.table_ref), custom_call_target="tpu_custom_call" | custom-call | tf_op jit(solution)/shard_map/reflux_moments/pallas_call | solution.py:515

commit v2 on v1

--- a/solution.py
+++ b/solution.py
@@ -16,7 +16,6 @@
 SHIFTS = (1, -1, 2, -2)
 VEC = (8, 128)
 ITEMS = 6
-BLOCK_ROWS = ITEMS * 8
 FINE_ROWS = 5 * 2 * 8
 
 
@@ -54,30 +53,27 @@
     return centroid_ref[field - 1, :, pl.ds(start, size)]
 
 
-def greet(count, me):
+def within(device, count):
+    return (device >= 0) & (device < count)
+
+
+def greet(me, peers):
     barrier = pltpu.get_barrier_semaphore()
-    for shift in SHIFTS:
-        other = me + shift
-
-        @pl.when((other >= 0) & (other < count))
+    number = 0
+    for other, there in peers:
+
+        @pl.when(there)
         def _signal():
             pl.semaphore_signal(
                 barrier, inc=1, device_id=(other,), device_id_type=pl.DeviceIdType.MESH
             )
 
-    peers = sum(
-        ((me + shift >= 0) & (me + shift < count)).astype(jnp.int32) for shift in SHIFTS
-    )
-    pl.semaphore_wait(barrier, peers)
-
-
-def each_neighbour(count, me, action):
-    for place, shift in enumerate(SHIFTS):
-        other = me + shift
-
-        @pl.when((other >= 0) & (other < count))
-        def _act():
-            action(place, shift, other)
+        number = number + there.astype(jnp.int32)
+    return barrier, number
+
+
+def direct_peers(me, count):
+    return [(me + shift, within(me + shift, count)) for shift in SHIFTS]
 
 
 def remote(src, dst, send, recv, other):
@@ -91,93 +87,185 @@
     )
 
 
+class Direct:
+    def __init__(self, me, count, buffer, pieces, send, recv):
+        self.me, self.count = me, count
+        self.buffer, self.pieces, self.send, self.recv = buffer, pieces, send, recv
+
+    def peers(self):
+        return direct_peers(self.me, self.count)
+
+    def copy(self, place, piece):
+        shift = SHIFTS[place]
+        return remote(
+            self.buffer.at[REACH, piece],
+            self.buffer.at[REACH - shift, piece],
+            self.send.at[place, piece],
+            self.recv.at[place, piece],
+            self.me + shift,
+        )
+
+    def start(self, piece):
+        for place, shift in enumerate(SHIFTS):
+            pl.when(within(self.me + shift, self.count))(self.copy(place, piece).start)
+
+    def forward(self, piece):
+        pass
+
+    def finish(self):
+        for piece in self.pieces:
+            for place, shift in enumerate(SHIFTS):
+                pl.when(within(self.me + shift, self.count))(self.copy(place, piece).wait_send)
+                pl.when(within(self.me - shift, self.count))(self.copy(place, piece).wait_recv)
+
+
+class Relay:
+    def __init__(self, me, count, buffer, pieces, send, recv):
+        self.me, self.buffer, self.pieces, self.send, self.recv = me, buffer, pieces, send, recv
+        core, x, y = me % 2, me // 2 % 2, me // 4 % 2
+        unlike = (x + y) % 2
+        self.x, self.core = x, core
+        spare = 2 * REACH + 2
+        self.by_z = unlike == 0
+        z_to, z_from = me + 8 - 16 * x, me - 8 + 16 * x
+        self.z_send = self.by_z & within(z_to, count)
+        self.z_recv = self.by_z & within(z_from, count)
+        self.second = (unlike == 1) | within(z_from, count)
+        self.others = [(me + 4 - 8 * y, me >= 0)] + [
+            (me + shift, self.by_z & within(me + shift, count)) for shift in (8, -8)
+        ]
+        y_there = unlike * spare + (1 - unlike) * 4 * x
+        y_here = (1 - unlike) * spare + unlike * 4 * x
+        self.steps = (
+            (me + 2 - 4 * x, REACH, 4 * x, 4 * (1 - x)),
+            (me + 1 - 2 * core, REACH, 1 + 2 * core, 3 - 2 * core),
+            (me + 4 - 8 * y, 4 * (1 - x), y_there, y_here),
+            (z_to, spare, 4 * x, 4 * x),
+            (me + 1 - 2 * core, 4 * (1 - core), 3 - 2 * core, 1 + 2 * core),
+        )
+
+    def peers(self):
+        near = [(self.steps[0][0], self.me >= 0), (self.steps[1][0], self.me >= 0)]
+        return near + self.others
+
+    def sent(self, step, piece):
+        other, source, there, _here = self.steps[step]
+        return remote(
+            self.buffer.at[source, piece],
+            self.buffer.at[there, piece],
+            self.send.at[step, piece],
+            self.recv.at[step, piece],
+            other,
+        )
+
+    def arrived(self, step, piece):
+        other, source, _there, here = self.steps[step]
+        return remote(
+            self.buffer.at[source, piece],
+            self.buffer.at[here, piece],
+            self.send.at[step, piece],
+            self.recv.at[step, piece],
+            other,
+        )
+
+    def start(self, piece):
+        self.sent(0, piece).start()
+        self.sent(1, piece).start()
+
+    def forward(self, piece):
+        self.arrived(0, piece).wait_recv()
+        self.sent(2, piece).start()
+        pl.when(self.x == self.core)(self.sent(4, piece).start)
+
+    def finish(self):
+        late = self.x != self.core
+        for piece in self.pieces:
+            self.arrived(2, piece).wait_recv()
+            pl.when(self.z_send)(self.sent(3, piece).start)
+            pl.when(jnp.logical_not(self.by_z) & late)(self.sent(4, piece).start)
+        for piece in self.pieces:
+
+            @pl.when(self.z_recv)
+            def _last():
+                self.arrived(3, piece).wait_recv()
+                pl.when(late)(self.sent(4, piece).start)
+
+        for piece in self.pieces:
+            self.arrived(1, piece).wait_recv()
+            pl.when(self.second | late)(self.arrived(4, piece).wait_recv)
+            for step in range(3):
+                self.sent(step, piece).wait_send()
+            pl.when(self.z_send)(self.sent(3, piece).wait_send)
+            pl.when(self.second | jnp.logical_not(late))(self.sent(4, piece).wait_send)
+
+
+def way(count):
+    return Relay if count == 32 else Direct
+
+
 def faces_kernel(
     count, fraction_ref, centroid_ref, refine_ref, near_ref, table_ref, send, recv, send2, recv2
 ):
     me = lax.axis_index("sfc")
-    near_own = REACH
+    order = (4, 5, 0, 1, 2, 3)
+    faces = way(count)(me, count, near_ref, order, send, recv)
+    peers = direct_peers(me, count)
+    if count == 32:
+        peers = peers + faces.others
+    barrier, number = greet(me, peers)
     swapped = edge_index(True)
     plain = edge_index(False)
 
-    def extract(slot, index, swap):
-        for field in range(4):
+    def extract(slot, item, index, swap):
+        if item < 4:
             for pair in range(8):
-                chunk = field_rows(fraction_ref, centroid_ref, field, pair * 512, 512)
+                chunk = field_rows(fraction_ref, centroid_ref, item, pair * 512, 512)
                 tiles = [chunk[:, 128 * t : 128 * t + 128] for t in range(4)]
-                near_ref[slot, pl.ds(field * 8 + pair, 8, stride=BLOCK_ROWS), :] = edges(
-                    tiles, index
-                )
+                near_ref[slot, item, pl.ds(pair, 8, stride=8), :] = edges(tiles, index)
+        else:
             for side in range(2):
-                start = (1 - side if swap else side) * 3840
-                for half in range(2):
-                    near_ref[
-                        slot, pl.ds(32 + half * 8 + side * 4 + field, 8, stride=BLOCK_ROWS), :
-                    ] = field_rows(fraction_ref, centroid_ref, field, start + half * 128, 128)
-
-    extract(near_own, swapped, True)
-    table_ref[near_own] = refine_ref[...]
-    greet(count, me)
-
-    def start(place, shift, other):
-        remote(
-            near_ref.at[near_own], near_ref.at[REACH - shift], send.at[place], recv.at[place], other
-        ).start()
-        remote(
-            refine_ref, table_ref.at[REACH - shift], send2.at[place], recv2.at[place], other
-        ).start()
-
-    each_neighbour(count, me, start)
-    extract(2 * REACH + 1, plain, False)
-
-    def finish_send(place, shift, other):
-        remote(
-            near_ref.at[near_own], near_ref.at[REACH - shift], send.at[place], recv.at[place], other
-        ).wait_send()
-        remote(
-            refine_ref, table_ref.at[REACH - shift], send2.at[place], recv2.at[place], other
-        ).wait_send()
-
-    def finish_recv(place, shift, other):
-        remote(
-            near_ref.at[near_own], near_ref.at[REACH - shift], send.at[place], recv.at[place], other
-        ).wait_recv()
-        remote(
-            refine_ref, table_ref.at[REACH - shift], send2.at[place], recv2.at[place], other
-        ).wait_recv()
-
-    each_neighbour(count, me, finish_send)
+                start = (1 - side if swap else side) * 3840 + (item - 4) * 128
+                for field in range(4):
+                    near_ref[slot, item, pl.ds(side * 4 + field, 8, stride=8), :] = field_rows(
+                        fraction_ref, centroid_ref, field, start, 128
+                    )
+
+    table_ref[REACH] = refine_ref[...]
+    for piece in order:
+        extract(REACH, piece, swapped, True)
+        if piece == order[0]:
+            pl.semaphore_wait(barrier, number)
+        faces.start(piece)
+
+    def table_copy(place):
+        shift = SHIFTS[place]
+        return remote(
+            refine_ref, table_ref.at[REACH - shift], send2.at[place], recv2.at[place], me + shift
+        )
+
     for place, shift in enumerate(SHIFTS):
-        other = me - shift
-
-        @pl.when((other >= 0) & (other < count))
-        def _recv():
-            finish_recv(place, shift, other)
+        pl.when(within(me + shift, count))(table_copy(place).start)
+    for piece in order:
+        faces.forward(piece)
+        extract(2 * REACH + 1, piece, plain, False)
+    faces.finish()
+    for place, shift in enumerate(SHIFTS):
+        pl.when(within(me + shift, count))(table_copy(place).wait_send)
+        pl.when(within(me - shift, count))(table_copy(place).wait_recv)
 
 
 def packets_kernel(count, own_ref, near_ref, send, recv):
     me = lax.axis_index("sfc")
-    greet(count, me)
+    pieces = range(own_ref.shape[0])
+    packets = way(count)(me, count, near_ref, pieces, send, recv)
+    barrier, number = greet(me, packets.peers())
     near_ref[REACH] = own_ref[...]
-
-    def start(place, shift, other):
-        remote(own_ref, near_ref.at[REACH - shift], send.at[place], recv.at[place], other).start()
-
-    each_neighbour(count, me, start)
-
-    def finish_send(place, shift, other):
-        remote(
-            own_ref, near_ref.at[REACH - shift], send.at[place], recv.at[place], other
-        ).wait_send()
-
-    each_neighbour(count, me, finish_send)
-    for place, shift in enumerate(SHIFTS):
-        other = me - shift
-
-        @pl.when((other >= 0) & (other < count))
-        def _recv():
-            remote(
-                own_ref, near_ref.at[REACH - shift], send.at[place], recv.at[place], other
-            ).wait_recv()
+    pl.semaphore_wait(barrier, number)
+    for piece in pieces:
+        packets.start(piece)
+    for piece in pieces:
+        packets.forward(piece)
+    packets.finish()
 
 
 def solve(h, g):
@@ -262,14 +350,18 @@
                     (2 * REACH + 1) * BLK + block,
                 )
             )
+
+        def face(k, item):
+            return near_ref[place[k] // BLK, item, place[k] % BLK]
+
         for field in range(4):
-            value = near_ref[place[5], field]
+            value = face(5, field)
             for k in (4, 3, 2):
-                value = jnp.where(lane < (k - 1) * 32, near_ref[place[k], field], value)
+                value = jnp.where(lane < (k - 1) * 32, face(k, field), value)
             ghost_edges[block * 32 + field * 8 : block * 32 + field * 8 + 8, :] = value
         for half in range(2):
             ghost_layers[half, block * 8 : block * 8 + 8, :] = jnp.where(
-                row < 4, near_ref[place[0], 4 + half], near_ref[place[1], 4 + half]
+                row < 4, face(0, 4 + half), face(1, 4 + half)
             )
 
     for field in range(4):
@@ -471,6 +563,7 @@
 def per_device(fraction, centroid, velocity, neighbours, refinement):
     count = lax.axis_size("sfc")
     slots = refinement.shape[0]
+    pieces = 4 if slots % 4 == 0 else 1
     vmem, smem = spec(pltpu.VMEM), spec(pltpu.SMEM)
     f32 = jnp.float32
     refinement = refinement.T
@@ -478,12 +571,13 @@
     near, table = pl.pallas_call(
         lambda *refs: faces_kernel(count, *refs),
         out_shape=(
-            jax.ShapeDtypeStruct((6, BLK * BLOCK_ROWS, 128), f32),
+            jax.ShapeDtypeStruct((7, ITEMS, BLK * 8, 128), f32),
             jax.ShapeDtypeStruct((5, 4, slots), jnp.int32),
         ),
         in_specs=[vmem] * 3,
         out_specs=(vmem, vmem),
-        scratch_shapes=[pltpu.SemaphoreType.DMA((4,))] * 4,
+        scratch_shapes=[pltpu.SemaphoreType.DMA((5, ITEMS))] * 2
+        + [pltpu.SemaphoreType.DMA((4,))] * 2,
         compiler_params=pltpu.CompilerParams(collective_id=0, has_side_effects=True),
         name="exchange_faces",
     )(fraction, centroid, refinement)
@@ -502,16 +596,16 @@
             pltpu.VMEM((2, 64, 128), f32),
         ],
         name="fit_planes",
-    )(fraction, centroid, velocity, near.reshape(48, ITEMS, 8, 128), neighbours, refinement)
+    )(fraction, centroid, velocity, near.reshape(7, ITEMS, BLK, 8, 128), neighbours, refinement)
     near_packets = pl.pallas_call(
         lambda *refs: packets_kernel(count, *refs),
-        out_shape=jax.ShapeDtypeStruct((5, slots, 8, 128), f32),
+        out_shape=jax.ShapeDtypeStruct((7, pieces, slots // pieces * 8, 128), f32),
         in_specs=[vmem],
         out_specs=vmem,
-        scratch_shapes=[pltpu.SemaphoreType.DMA((4,))] * 2,
+        scratch_shapes=[pltpu.SemaphoreType.DMA((5, pieces))] * 2,
         compiler_params=pltpu.CompilerParams(collective_id=1, has_side_effects=True),
         name="exchange_packets",
-    )(packets)
+    )(packets.reshape(pieces, slots // pieces * 8, 128))
     reflux = pl.pallas_call(
         flux_kernel,
         out_shape=jax.ShapeDtypeStruct((BLK, 6, 2, 256), f32),
@@ -519,7 +613,7 @@
         out_specs=vmem,
         scratch_shapes=[pltpu.SMEM((5 * slots + 4,), jnp.int32)],
         name="reflux_moments",
-    )(faces, near_packets, table)
+    )(faces, near_packets.reshape(7, slots, 8, 128), table)
     return planes, reflux
 
 

time: 50.1 us -> 51.1 us (1.020); the launches traced: 49.2 us -> 50.9 us
  Pallas kernels: 48.6 us -> 50.2 us
    pallas_call x1, Pallas kernels: 8.69 us -> 13.2 us  [per_device(): pl.pallas_call(lambda *refs: packets_kernel(count, *refs), out_shape=jax....]
    pallas_call x1, Pallas kernels: 20.6 us -> 17.4 us  [per_device(): pl.pallas_call(lambda *refs: faces_kernel(count, *refs), out_shape=(jax.S...]
where the time goes in v2:
time: 51.1 us; the launch traced here: 50.9 us
  Pallas kernels  50.2 us (98%)
  between operations  0.65 us (1%)
    pallas_call x1, Pallas kernels, per_device(): pl.pallas_call(lambda *refs: faces_kernel(count, *refs), out_shape=(jax.S...  17.4 us
    pallas_call x1, Pallas kernels, per_device(): pl.pallas_call(fit_kernel, out_shape=(jax.ShapeDtypeStruct((BLK, 4, CELLS...  16.1 us
    pallas_call x1, Pallas kernels, per_device(): pl.pallas_call(lambda *refs: packets_kernel(count, *refs), out_shape=jax....  13.2 us
    pallas_call x1, Pallas kernels, per_device(): pl.pallas_call(flux_kernel, out_shape=jax.ShapeDtypeStruct((BLK, 6, 2, 25...  3.47 us

profile of v2, /device:TPU:0, one launch (start us, length us, event | category | flops | bytes accessed | tf_op | source)
XLA Modules:
  0.0 50.9 jit_solution(7718422771495263932)
XLA Ops:
  0.6 17.4 %exchange_faces.1 = (f32[7,6,64,128]{3,2,1,0:T(8,128)}, s32[5,4,16]{2,1,0:T(4,128)}) custom-call(f32[8,4096]{1,0:T(8,128)} %fraction_ref.1, f32[3,8,4096]{2,1,0:T(8,128)} %bitcast.7, s32[4,16]{1,0:T(4,128)} %bitcast.12), custom_call_target="tpu_custom_call" | custom-call | tf_op jit(solution)/shard_map/exchange_faces/pallas_call | solution.py:571
  18.0 16.1 %fit_planes.1 = (f32[8,4,4096]{2,1,0:T(4,128)}, f32[640,128]{1,0:T(8,128)}, f32[16,8,128]{2,1,0:T(8,128)}) custom-call(f32[8,4096]{1,0:T(8,128)} %fraction_ref.1, f32[3,8,4096]{2,1,0:T(8,128)} %bitcast.8, f32[3,8,4096]{2,1,0:T(8,128)} %bitcast.10, f32[7,6,8,8,128]{4,3,2,1,0:T(8,128)} %bitcast.9, s32[8,6]{1,0:T(8,128)} %neighbours_ref.1, s32[4,16]{1,0:T(4,128)} %bitcast.13), custom_call_target="tpu_custom_call" | custom-call | tf_op jit(solution)/shard_map/fit_planes/pallas_call | solution.py:584
  34.2 13.2 %exchange_packets.1 = f32[7,4,32,128]{3,2,1,0:T(8,128)} custom-call(f32[4,32,128]{2,1,0:T(8,128)} %bitcast.11), custom_call_target="tpu_custom_call" | custom-call | tf_op jit(solution)/shard_map/exchange_packets/pallas_call | solution.py:600
  47.4 3.5 %reflux_moments.1 = f32[8,6,2,256]{3,2,1,0:T(2,128)} custom-call(f32[640,128]{1,0:T(8,128)} %get-tuple-element.9.faces_ref, f32[7,16,8,128]{3,2,1,0:T(8,128)} %bitcast.6, s32[5,4,16]{2,1,0:T(4,128)} %get-tuple-element.11.table_ref), custom_call_target="tpu_custom_call" | custom-call | tf_op jit(solution)/shard_map/reflux_moments/pallas_call | solution.py:609

commit v3 on v2

--- a/solution.py
+++ b/solution.py
@@ -1,5 +1,6 @@
 import jax
 import jax.numpy as jnp
+import numpy as np
 from jax import lax
 from jax.experimental import pallas as pl
 from jax.experimental.pallas import tpu as pltpu
@@ -16,7 +17,7 @@
 SHIFTS = (1, -1, 2, -2)
 VEC = (8, 128)
 ITEMS = 6
-FINE_ROWS = 5 * 2 * 8
+FINE_ROWS = 4 * 2 * 8
 
 
 def lanes():
@@ -27,24 +28,42 @@
     return jnp.take_along_axis(values, index, axis=1, mode="promise_in_bounds")
 
 
-def edge_index(swap):
-    lane = lanes()
-    kind = lane // 32
-    if swap:
-        kind = kind + 1 - 2 * (kind % 2)
-    j = lane % 16
-    source = jnp.where(
-        kind == 0, j, jnp.where(kind == 1, 112 + j, (j % 8) * 16 + jnp.where(kind == 3, 15, 0))
-    )
-    upper = jnp.where(kind == 0, 0, jnp.where(kind == 1, 1, j // 8))
-    return source, upper == 1, (lane // 16) % 2 == 1
-
-
-def edges(tiles, index):
-    source, upper, odd = index
-    first = jnp.where(upper, take(tiles[1], source), take(tiles[0], source))
-    second = jnp.where(upper, take(tiles[3], source), take(tiles[2], source))
-    return jnp.where(odd, second, first)
+def edge_place(kind, odd, j):
+    y, z = ((0, j), (15, j), (j, 0), (j, 15))[kind]
+    return odd * 256 + y * 16 + z
+
+
+def edge_matrix():
+    matrix = np.zeros((512, 256), np.float32)
+    for lane in range(128):
+        kind, odd, j = lane // 32, lane // 16 % 2, lane % 16
+        matrix[edge_place(kind + 1 - 2 * (kind % 2), odd, j), lane] = 1
+        matrix[edge_place(kind, odd, j), 128 + lane] = 1
+    return jnp.asarray(matrix, jnp.bfloat16)
+
+
+def ghost_matrix():
+    matrix = np.zeros((128, 512), np.float32)
+    for lane in range(64, 128):
+        matrix[lane, edge_place(lane // 32, lane // 16 % 2, lane % 16)] = 1
+    return jnp.asarray(matrix, jnp.bfloat16)
+
+
+def select(values, matrix):
+    high = values.astype(jnp.bfloat16)
+    rest = values - high.astype(jnp.float32)
+    middle = rest.astype(jnp.bfloat16)
+    low = (rest - middle.astype(jnp.float32)).astype(jnp.bfloat16)
+    parts = [
+        jnp.dot(part, matrix, preferred_element_type=jnp.float32) for part in (low, middle, high)
+    ]
+    return parts[0] + parts[1] + parts[2]
+
+
+def layer_parts(low, high, part):
+    first = low if part == 0 else pltpu.roll(low, 128 - 32 * part, 1)
+    second = high if part == 1 else pltpu.roll(high, (160 - 32 * part) % 128, 1)
+    return jnp.where(lanes() < 32, first, second)
 
 
 def field_rows(fraction_ref, centroid_ref, field, start, size):
@@ -204,7 +223,19 @@
 
 
 def faces_kernel(
-    count, fraction_ref, centroid_ref, refine_ref, near_ref, table_ref, send, recv, send2, recv2
+    count,
+    fraction_ref,
+    centroid_ref,
+    velocity_ref,
+    refine_ref,
+    edge_ref,
+    near_ref,
+    table_ref,
+    speed_ref,
+    send,
+    recv,
+    send2,
+    recv2,
 ):
     me = lax.axis_index("sfc")
     order = (4, 5, 0, 1, 2, 3)
@@ -213,29 +244,42 @@
     if count == 32:
         peers = peers + faces.others
     barrier, number = greet(me, peers)
-    swapped = edge_index(True)
-    plain = edge_index(False)
-
-    def extract(slot, item, index, swap):
-        if item < 4:
-            for pair in range(8):
-                chunk = field_rows(fraction_ref, centroid_ref, item, pair * 512, 512)
-                tiles = [chunk[:, 128 * t : 128 * t + 128] for t in range(4)]
-                near_ref[slot, item, pl.ds(pair, 8, stride=8), :] = edges(tiles, index)
-        else:
-            for side in range(2):
-                start = (1 - side if swap else side) * 3840 + (item - 4) * 128
-                for field in range(4):
-                    near_ref[slot, item, pl.ds(side * 4 + field, 8, stride=8), :] = field_rows(
-                        fraction_ref, centroid_ref, field, start, 128
-                    )
-
-    table_ref[REACH] = refine_ref[...]
-    for piece in order:
-        extract(REACH, piece, swapped, True)
-        if piece == order[0]:
-            pl.semaphore_wait(barrier, number)
-        faces.start(piece)
+
+    def extract_layers(slot, item, swap):
+        for side in range(2):
+            start = (1 - side if swap else side) * 3840 + (item - 4) * 128
+            for field in range(4):
+                near_ref[slot, item, pl.ds(side * 4 + field, 8, stride=8), :] = field_rows(
+                    fraction_ref, centroid_ref, field, start, 128
+                )
+
+    extract_layers(REACH, 4, True)
+    extract_layers(REACH, 5, True)
+    pl.semaphore_wait(barrier, number)
+    faces.start(4)
+    faces.start(5)
+    both = select(
+        jnp.concatenate(
+            [
+                field_rows(fraction_ref, centroid_ref, field, pair * 512, 512)
+                for field in range(4)
+                for pair in range(8)
+            ],
+            0,
+        ),
+        edge_ref[...],
+    )
+
+    def put(slot, field, start):
+        for pair in range(8):
+            row = field * 64 + pair * 8
+            near_ref[slot, field, pl.ds(pair, 8, stride=8), :] = both[
+                row : row + 8, start : start + 128
+            ]
+
+    for field in range(4):
+        put(REACH, field, 0)
+        faces.start(field)
 
     def table_copy(place):
         shift = SHIFTS[place]
@@ -243,11 +287,38 @@
             refine_ref, table_ref.at[REACH - shift], send2.at[place], recv2.at[place], me + shift
         )
 
+    table_ref[REACH] = refine_ref[...]
     for place, shift in enumerate(SHIFTS):
         pl.when(within(me + shift, count))(table_copy(place).start)
-    for piece in order:
-        faces.forward(piece)
-        extract(2 * REACH + 1, piece, plain, False)
+
+    for field in range(4):
+        put(2 * REACH + 1, field, 128)
+    faces.forward(4)
+    extract_layers(2 * REACH + 1, 4, False)
+    faces.forward(5)
+    extract_layers(2 * REACH + 1, 5, False)
+    faces.forward(0)
+    speeds = select(
+        jnp.concatenate(
+            [velocity_ref[axis, :, pl.ds(pair * 512, 512)] for axis in (1, 2) for pair in range(8)],
+            0,
+        ),
+        edge_ref[:, 128:],
+    )
+    for pair in range(8):
+        speed_ref[pl.ds(8 + pair, 8, stride=16), :] = jnp.where(
+            lanes() < 64, speeds[pair * 8 : pair * 8 + 8], speeds[64 + pair * 8 : 72 + pair * 8]
+        )
+    faces.forward(1)
+    for part in range(8):
+        start = part // 4 * 128
+        speed_ref[pl.ds(part, 8, stride=16), :] = layer_parts(
+            velocity_ref[0, :, start : start + 128],
+            velocity_ref[0, :, 3840 + start : 3968 + start],
+            part % 4,
+        )
+    faces.forward(2)
+    faces.forward(3)
     faces.finish()
     for place, shift in enumerate(SHIFTS):
         pl.when(within(me + shift, count))(table_copy(place).wait_send)
@@ -257,7 +328,7 @@
 def packets_kernel(count, own_ref, near_ref, send, recv):
     me = lax.axis_index("sfc")
     pieces = range(own_ref.shape[0])
-    packets = way(count)(me, count, near_ref, pieces, send, recv)
+    packets = Direct(me, count, near_ref, pieces, send, recv)
     barrier, number = greet(me, packets.peers())
     near_ref[REACH] = own_ref[...]
     pl.semaphore_wait(barrier, number)
@@ -323,7 +394,9 @@
 def fit_kernel(
     fraction_ref,
     centroid_ref,
-    velocity_ref,
+    speed_ref,
+    edge_ref,
+    ghost_ref,
     near_ref,
     neighbours_ref,
     refine_ref,
@@ -333,6 +406,8 @@
     padded,
     ghost_edges,
     ghost_layers,
+    ghost_z_cells,
+    layers,
 ):
     me = lax.axis_index("sfc")
     lane = lanes()
@@ -376,14 +451,13 @@
     wide = lax.broadcasted_iota(jnp.int32, (8, 512), 1)
     y_pos = wide // 16 % 16
     z_pos = wide % 16
-    plain = edge_index(False)
-    y_source, z_source = [], []
+    z_cells = select(ghost_edges[...], ghost_ref[...])
     for tile in range(4):
-        odd, upper = tile // 2, tile % 2
-        y_source.append(upper * 32 + odd * 16 + lane % 16)
-        z_source.append(
-            jnp.where(lane % 16 < 8, 64, 96) + odd * 16 + upper * 8 + lane // 16
-        )
+        ghost_z_cells[tile] = z_cells[:, tile * 128 : tile * 128 + 128]
+
+    def side_ghosts(ghost):
+        shifts = (0, 80, 112, 64)
+        return jnp.concatenate([pltpu.roll(ghost, i, 1) if i else ghost for i in shifts], 1)
 
     def one_pair(pair, carry):
         start = pl.multiple_of(pair * 512, 512)
@@ -391,8 +465,10 @@
         for field in range(4):
             center = padded[field, :, pl.ds(start + 256, 512)]
             ghost = ghost_edges[pl.ds(field * 8 + pair, 8, stride=32), :]
-            ghost_y = jnp.concatenate([take(ghost, i) for i in y_source], 1)
-            ghost_z = jnp.concatenate([take(ghost, i) for i in z_source], 1)
+            ghost_y = side_ghosts(ghost)
+            ghost_z = jnp.concatenate(
+                [ghost_z_cells[i, pl.ds(field * 8 + pair, 8, stride=32), :] for i in range(4)], 1
+            )
             fields[0].append(center)
             fields[1].append(padded[field, :, pl.ds(start, 512)])
             fields[2].append(padded[field, :, pl.ds(start + 512, 512)])
@@ -411,34 +487,26 @@
         params = fit(points, (a, b, c, d))
         for comp in range(4):
             planes_ref[:, comp, pl.ds(start, 512)] = params[comp]
-            tiles = [params[comp][:, 128 * t : 128 * t + 128] for t in range(4)]
-            fine_table[pl.ds(comp * 16 + 8 + pair, 8, stride=FINE_ROWS), :] = edges(tiles, plain)
-        speeds = []
-        for axis in (1, 2):
-            chunk = velocity_ref[axis, :, pl.ds(start, 512)]
-            speeds.append(edges([chunk[:, 128 * t : 128 * t + 128] for t in range(4)], plain))
-        fine_table[pl.ds(4 * 16 + 8 + pair, 8, stride=FINE_ROWS), :] = jnp.where(
-            lane < 64, speeds[0], speeds[1]
-        )
+            layers[pl.ds(pl.multiple_of(pair * 32 + comp * 8, 8), 8), :] = params[comp]
         return carry
 
     lax.fori_loop(0, 8, one_pair, 0)
 
-    for comp in range(5):
-        for half in range(2):
-            sides = []
-            for side in range(2):
-                start = side * 3840 + half * 128
-                if comp < 4:
-                    sides.append(planes_ref[:, comp, start : start + 128])
-                else:
-                    sides.append(velocity_ref[0, :, start : start + 128])
-            for part in range(4):
-                low = sides[0] if part == 0 else pltpu.roll(sides[0], 128 - 32 * part, 1)
-                high = sides[1] if part == 1 else pltpu.roll(sides[1], (160 - 32 * part) % 128, 1)
-                fine_table[pl.ds(comp * 16 + half * 4 + part, 8, stride=FINE_ROWS), :] = jnp.where(
-                    lane < 32, low, high
-                )
+    edge_values = select(layers[...], edge_ref[:, 128:])
+    for pair in range(8):
+        for comp in range(4):
+            row_at = pair * 32 + comp * 8
+            fine_table[pl.ds(comp * 16 + 8 + pair, 8, stride=FINE_ROWS), :] = edge_values[
+                row_at : row_at + 8
+            ]
+    for comp in range(4):
+        for part in range(8):
+            start = part // 4 * 128
+            fine_table[pl.ds(comp * 16 + part, 8, stride=FINE_ROWS), :] = layer_parts(
+                layers[comp * 8 : comp * 8 + 8, start : start + 128],
+                layers[224 + comp * 8 : 232 + comp * 8, 256 + start : 384 + start],
+                part % 4,
+            )
 
     for slot in range(refine_ref.shape[1]):
         block = jnp.clip(refine_ref[0, slot] - me * BLK, 0, BLK - 1)
@@ -447,15 +515,19 @@
         base = block * FINE_ROWS + yz * 8
         group = k - 2 * yz
         parts = []
-        for target, comp in enumerate((k // 2, 3, 4)):
-            value = fine_table[pl.ds(pl.multiple_of(base + comp * 16, 8), 8), :]
+        for target in range(3):
+            if target < 2:
+                comp = (k // 2, 3)[target]
+                value = fine_table[pl.ds(pl.multiple_of(base + comp * 16, 8), 8), :]
+            else:
+                value = speed_ref[pl.ds(pl.multiple_of(block * 16 + yz * 8, 8), 8), :]
             parts.append(pltpu.roll(value, (128 + 32 * target - 32 * group) % 128, 1))
         packets_ref[slot] = jnp.where(
             lane < 32, parts[0], jnp.where(lane < 64, parts[1], parts[2])
         )
 
 
-def flux_kernel(faces_ref, packets_ref, table_ref, reflux_ref, live_list):
+def flux_kernel(faces_ref, speed_ref, packets_ref, table_ref, reflux_ref, live_list):
     me = lax.axis_index("sfc")
     lane = lanes()
     row = lax.broadcasted_iota(jnp.int32, VEC, 0)
@@ -499,17 +571,16 @@
         base = block * FINE_ROWS + yz * 8
         first = jnp.where(axis == 0, 1, 0)
         second = jnp.where(axis == 2, 1, 2)
+        sources = [
+            faces_ref[pl.ds(pl.multiple_of(base + comp * 16, 8), 8), :]
+            for comp in (axis, first, second, 3)
+        ]
+        sources.append(speed_ref[pl.ds(pl.multiple_of(block * 16 + yz * 8, 8), 8), :])
         normal_c, one_c, two_c, d_c, u_c = [
             take(
-                jnp.take_along_axis(
-                    faces_ref[pl.ds(pl.multiple_of(base + comp * 16, 8), 8), :],
-                    from_row,
-                    axis=0,
-                    mode="promise_in_bounds",
-                ),
-                from_lane,
-            )
-            for comp in (axis, first, second, 3, 4)
+                jnp.take_along_axis(source, from_row, axis=0, mode="promise_in_bounds"), from_lane
+            )
+            for source in sources
         ]
         packet = packets_ref[offset, slot]
         normal_f = packet
@@ -568,19 +639,21 @@
     f32 = jnp.float32
     refinement = refinement.T
     centroid, velocity = jnp.swapaxes(centroid, 0, 1), jnp.swapaxes(velocity, 0, 1)
-    near, table = pl.pallas_call(
+    edge = edge_matrix()
+    near, table, speeds = pl.pallas_call(
         lambda *refs: faces_kernel(count, *refs),
         out_shape=(
             jax.ShapeDtypeStruct((7, ITEMS, BLK * 8, 128), f32),
             jax.ShapeDtypeStruct((5, 4, slots), jnp.int32),
+            jax.ShapeDtypeStruct((BLK * 16, 128), f32),
         ),
-        in_specs=[vmem] * 3,
-        out_specs=(vmem, vmem),
+        in_specs=[vmem] * 5,
+        out_specs=(vmem,) * 3,
         scratch_shapes=[pltpu.SemaphoreType.DMA((5, ITEMS))] * 2
         + [pltpu.SemaphoreType.DMA((4,))] * 2,
         compiler_params=pltpu.CompilerParams(collective_id=0, has_side_effects=True),
         name="exchange_faces",
-    )(fraction, centroid, refinement)
+    )(fraction, centroid, velocity, refinement, edge)
     planes, faces, packets = pl.pallas_call(
         fit_kernel,
         out_shape=(
@@ -588,15 +661,26 @@
             jax.ShapeDtypeStruct((BLK * FINE_ROWS, 128), f32),
             jax.ShapeDtypeStruct((slots, 8, 128), f32),
         ),
-        in_specs=[vmem] * 4 + [smem] * 2,
+        in_specs=[vmem] * 6 + [smem] * 2,
         out_specs=(vmem,) * 3,
         scratch_shapes=[
             pltpu.VMEM((4, 8, CELLS + 512), f32),
             pltpu.VMEM((256, 128), f32),
             pltpu.VMEM((2, 64, 128), f32),
+            pltpu.VMEM((4, 256, 128), f32),
+            pltpu.VMEM((256, 512), f32),
         ],
         name="fit_planes",
-    )(fraction, centroid, velocity, near.reshape(7, ITEMS, BLK, 8, 128), neighbours, refinement)
+    )(
+        fraction,
+        centroid,
+        speeds,
+        edge,
+        ghost_matrix(),
+        near.reshape(7, ITEMS, BLK, 8, 128),
+        neighbours,
+        refinement,
+    )
     near_packets = pl.pallas_call(
         lambda *refs: packets_kernel(count, *refs),
         out_shape=jax.ShapeDtypeStruct((7, pieces, slots // pieces * 8, 128), f32),
@@ -609,11 +693,11 @@
     reflux = pl.pallas_call(
         flux_kernel,
         out_shape=jax.ShapeDtypeStruct((BLK, 6, 2, 256), f32),
-        in_specs=[vmem] * 2 + [smem],
+        in_specs=[vmem] * 3 + [smem],
         out_specs=vmem,
         scratch_shapes=[pltpu.SMEM((5 * slots + 4,), jnp.int32)],
         name="reflux_moments",
-    )(faces, near_packets.reshape(7, slots, 8, 128), table)
+    )(faces, speeds, near_packets.reshape(7, slots, 8, 128), table)
     return planes, reflux
 
 

time: 51.1 us -> 48.2 us (0.943)
  the two profiles are of different devices: /device:TPU:0 before, /device:TPU:19 now
where the time goes in v3:
time: 48.2 us
  Pallas kernels  47.6 us (99%)
  between operations  0.65 us (1%)
    pallas_call x1, Pallas kernels, per_device(): pl.pallas_call(fit_kernel, out_shape=(jax.ShapeDtypeStruct((BLK, 4, CELLS...  15.5 us
    pallas_call x1, Pallas kernels, per_device(): pl.pallas_call(lambda *refs: faces_kernel(count, *refs), out_shape=(jax.S...  15 us
    pallas_call x1, Pallas kernels, per_device(): pl.pallas_call(lambda *refs: packets_kernel(count, *refs), out_shape=jax....  12.6 us
    pallas_call x1, Pallas kernels, per_device(): pl.pallas_call(flux_kernel, out_shape=jax.ShapeDtypeStruct((BLK, 6, 2, 25...  4.5 us

profile of v3, /device:TPU:19, one launch (start us, length us, event | category | flops | bytes accessed | tf_op | source)
XLA Modules:
  0.0 48.2 jit_solution(10188201687476547358)
XLA Ops:
  0.6 15.0 %exchange_faces.1 = (f32[7,6,64,128]{3,2,1,0:T(8,128)}, s32[5,4,16]{2,1,0:T(4,128)}, f32[128,128]{1,0:T(8,128)}) custom-call(f32[8,4096]{1,0:T(8,128)} %fraction_ref.1, f32[3,8,4096]{2,1,0:T(8,128)} %bitcast.7, f32[3,8,4096]{2,1,0:T(8,128)} %bitcast.10, s32[4,16]{1,0:T(4,128)} %bitcast.12, bf16[512,256]{1,0:T(8,128)(2,1)} %constant.4.clone.refs_4_.edge_ref), custom_call_target="tpu_custom_call" | custom-call | tf_op jit(solution)/shard_map/exchange_faces/pallas_call | solution.py:643
  15.7 15.5 %fit_planes.1 = (f32[8,4,4096]{2,1,0:T(4,128)}, f32[512,128]{1,0:T(8,128)}, f32[16,8,128]{2,1,0:T(8,128)}) custom-call(f32[8,4096]{1,0:T(8,128)} %fraction_ref.1, f32[3,8,4096]{2,1,0:T(8,128)} %bitcast.8, f32[128,128]{1,0:T(8,128)} %get-tuple-element.8.speed_ref, bf16[512,256]{1,0:T(8,128)(2,1)} %constant.4.clone.refs_4_.edge_ref, ...), custom_call_target="tpu_custom_call" | custom-call | tf_op jit(solution)/shard_map/fit_planes/pallas_call | solution.py:657
  31.2 12.6 %exchange_packets.1 = f32[7,4,32,128]{3,2,1,0:T(8,128)} custom-call(f32[4,32,128]{2,1,0:T(8,128)} %bitcast.11), custom_call_target="tpu_custom_call" | custom-call | tf_op jit(solution)/shard_map/exchange_packets/pallas_call | solution.py:684
  43.7 4.5 %reflux_moments.1 = f32[8,6,2,256]{3,2,1,0:T(2,128)} custom-call(f32[512,128]{1,0:T(8,128)} %get-tuple-element.11.faces_ref, f32[128,128]{1,0:T(8,128)} %get-tuple-element.8.speed_ref, f32[7,16,8,128]{3,2,1,0:T(8,128)} %bitcast.6, s32[5,4,16]{2,1,0:T(4,128)} %get-tuple-element.13.table_ref), custom_call_target="tpu_custom_call" | custom-call | tf_op jit(solution)/shard_map/reflux_moments/pallas_call | solution.py:693

commit v4 on v3

--- a/solution.py
+++ b/solution.py
@@ -189,26 +189,36 @@
 
     def start(self, piece):
         self.sent(0, piece).start()
-        self.sent(1, piece).start()
 
     def forward(self, piece):
-        self.arrived(0, piece).wait_recv()
-        self.sent(2, piece).start()
-        pl.when(self.x == self.core)(self.sent(4, piece).start)
-
-    def finish(self):
+        at = self.pieces.index(piece)
+        self.hand_on(at, at - 1, at - 2)
+
+    def hand_on(self, by_x, by_y, by_z):
         late = self.x != self.core
-        for piece in self.pieces:
+        if 0 <= by_x < len(self.pieces):
+            piece = self.pieces[by_x]
+            self.arrived(0, piece).wait_recv()
+            self.sent(2, piece).start()
+            pl.when(jnp.logical_not(late))(self.sent(4, piece).start)
+            self.sent(1, piece).start()
+        if 0 <= by_y < len(self.pieces):
+            piece = self.pieces[by_y]
             self.arrived(2, piece).wait_recv()
             pl.when(self.z_send)(self.sent(3, piece).start)
             pl.when(jnp.logical_not(self.by_z) & late)(self.sent(4, piece).start)
-        for piece in self.pieces:
+        if 0 <= by_z < len(self.pieces):
+            piece = self.pieces[by_z]
 
             @pl.when(self.z_recv)
             def _last():
                 self.arrived(3, piece).wait_recv()
                 pl.when(late)(self.sent(4, piece).start)
 
+    def finish(self):
+        late = self.x != self.core
+        for at in range(len(self.pieces), len(self.pieces) + 2):
+            self.hand_on(at, at - 1, at - 2)
         for piece in self.pieces:
             self.arrived(1, piece).wait_recv()
             pl.when(self.second | late)(self.arrived(4, piece).wait_recv)
@@ -293,10 +303,10 @@
 
     for field in range(4):
         put(2 * REACH + 1, field, 128)
+    extract_layers(2 * REACH + 1, 4, False)
+    extract_layers(2 * REACH + 1, 5, False)
     faces.forward(4)
-    extract_layers(2 * REACH + 1, 4, False)
     faces.forward(5)
-    extract_layers(2 * REACH + 1, 5, False)
     faces.forward(0)
     speeds = select(
         jnp.concatenate(
@@ -363,15 +373,18 @@
 
 
 def fit(points, params):
-    def one_pass(_unused, params):
-        a, b, c, d = params
+    width = 256
+
+    def normal_equations(start, params):
+        a, b, c, d = [p[:, start : start + width] for p in params]
         h = [None] * 10
         g = [None] * 4
 
         def add(total, place, term):
             total[place] = term if total[place] is None else total[place] + term
 
-        for px, py, pz, f in points:
+        for point in points:
+            px, py, pz, f = [value[:, start : start + width] for value in point]
             t = jnp.tanh(a * px + b * py + c * pz + d)
             s = 1.0 - t * t
             q = s * s
@@ -385,7 +398,12 @@
                 add(g, place, term)
         for place in (0, 4, 7, 9):
             h[place] = h[place] + 4.0 * DAMPING
-        step = solve(h, g)
+        return h + g
+
+    def one_pass(_unused, params):
+        parts = [normal_equations(start, params) for start in range(0, 512, width)]
+        sums = [jnp.concatenate(part, 1) for part in zip(*parts)]
+        step = solve(sums[:10], sums[10:])
         return tuple(p - s for p, s in zip(params, step))
 
     return lax.fori_loop(0, PASSES, one_pass, params)

time: 48.2 us -> 54.6 us (1.13)
  the two profiles are of different devices: /device:TPU:19 before, /device:TPU:11 now
where the time goes in v4:
time: 54.6 us; the launch traced here: 54.4 us
  Pallas kernels  53.7 us (98%)
  between operations  0.65 us (1%)
    pallas_call x1, Pallas kernels, per_device(): pl.pallas_call(lambda *refs: faces_kernel(count, *refs), out_shape=(jax.S...  22.8 us
    pallas_call x1, Pallas kernels, per_device(): pl.pallas_call(fit_kernel, out_shape=(jax.ShapeDtypeStruct((BLK, 4, CELLS...  14.7 us
    pallas_call x1, Pallas kernels, per_device(): pl.pallas_call(lambda *refs: packets_kernel(count, *refs), out_shape=jax....  12.3 us
    pallas_call x1, Pallas kernels, per_device(): pl.pallas_call(flux_kernel, out_shape=jax.ShapeDtypeStruct((BLK, 6, 2, 25...  3.99 us

profile of v4, /device:TPU:11, one launch (start us, length us, event | category | flops | bytes accessed | tf_op | source)
XLA Modules:
  0.0 54.4 jit_solution(13274154241773099470)
XLA Ops:
  0.6 22.8 %exchange_faces.1 = (f32[7,6,64,128]{3,2,1,0:T(8,128)}, s32[5,4,16]{2,1,0:T(4,128)}, f32[128,128]{1,0:T(8,128)}) custom-call(f32[8,4096]{1,0:T(8,128)} %fraction_ref.1, f32[3,8,4096]{2,1,0:T(8,128)} %bitcast.7, f32[3,8,4096]{2,1,0:T(8,128)} %bitcast.10, s32[4,16]{1,0:T(4,128)} %bitcast.12, bf16[512,256]{1,0:T(8,128)(2,1)} %constant.4.clone.refs_4_.edge_ref), custom_call_target="tpu_custom_call" | custom-call | tf_op jit(solution)/shard_map/exchange_faces/pallas_call | solution.py:661
  23.4 14.7 %fit_planes.1 = (f32[8,4,4096]{2,1,0:T(4,128)}, f32[512,128]{1,0:T(8,128)}, f32[16,8,128]{2,1,0:T(8,128)}) custom-call(f32[8,4096]{1,0:T(8,128)} %fraction_ref.1, f32[3,8,4096]{2,1,0:T(8,128)} %bitcast.8, f32[128,128]{1,0:T(8,128)} %get-tuple-element.8.speed_ref, bf16[512,256]{1,0:T(8,128)(2,1)} %constant.4.clone.refs_4_.edge_ref, ...), custom_call_target="tpu_custom_call" | custom-call | tf_op jit(solution)/shard_map/fit_planes/pallas_call | solution.py:675
  38.1 12.3 %exchange_packets.1 = f32[7,4,32,128]{3,2,1,0:T(8,128)} custom-call(f32[4,32,128]{2,1,0:T(8,128)} %bitcast.11), custom_call_target="tpu_custom_call" | custom-call | tf_op jit(solution)/shard_map/exchange_packets/pallas_call | solution.py:702
  50.4 4.0 %reflux_moments.1 = f32[8,6,2,256]{3,2,1,0:T(2,128)} custom-call(f32[512,128]{1,0:T(8,128)} %get-tuple-element.11.faces_ref, f32[128,128]{1,0:T(8,128)} %get-tuple-element.8.speed_ref, f32[7,16,8,128]{3,2,1,0:T(8,128)} %bitcast.6, s32[5,4,16]{2,1,0:T(4,128)} %get-tuple-element.13.table_ref), custom_call_target="tpu_custom_call" | custom-call | tf_op jit(solution)/shard_map/reflux_moments/pallas_call | solution.py:711

commit v5 on v4

--- a/solution.py
+++ b/solution.py
@@ -128,9 +128,6 @@
         for place, shift in enumerate(SHIFTS):
             pl.when(within(self.me + shift, self.count))(self.copy(place, piece).start)
 
-    def forward(self, piece):
-        pass
-
     def finish(self):
         for piece in self.pieces:
             for place, shift in enumerate(SHIFTS):
@@ -140,96 +137,59 @@
 
 class Relay:
     def __init__(self, me, count, buffer, pieces, send, recv):
-        self.me, self.buffer, self.pieces, self.send, self.recv = me, buffer, pieces, send, recv
-        core, x, y = me % 2, me // 2 % 2, me // 4 % 2
-        unlike = (x + y) % 2
-        self.x, self.core = x, core
-        spare = 2 * REACH + 2
-        self.by_z = unlike == 0
-        z_to, z_from = me + 8 - 16 * x, me - 8 + 16 * x
-        self.z_send = self.by_z & within(z_to, count)
-        self.z_recv = self.by_z & within(z_from, count)
-        self.second = (unlike == 1) | within(z_from, count)
-        self.others = [(me + 4 - 8 * y, me >= 0)] + [
-            (me + shift, self.by_z & within(me + shift, count)) for shift in (8, -8)
-        ]
-        y_there = unlike * spare + (1 - unlike) * 4 * x
-        y_here = (1 - unlike) * spare + unlike * 4 * x
+        self.buffer, self.pieces, self.send, self.recv = buffer, pieces, send, recv
+        core, x = me % 2, me // 2 % 2
+        to, origin = me + 4 - 8 * x, me - 4 + 8 * x
+        self.late = x != core
+        self.onward, self.second = within(to, count), within(origin, count)
+        self.others = [(me + shift, within(me + shift, count)) for shift in (4, -4)]
         self.steps = (
             (me + 2 - 4 * x, REACH, 4 * x, 4 * (1 - x)),
             (me + 1 - 2 * core, REACH, 1 + 2 * core, 3 - 2 * core),
-            (me + 4 - 8 * y, 4 * (1 - x), y_there, y_here),
-            (z_to, spare, 4 * x, 4 * x),
+            (to, 4 * (1 - x), 4 * x, 4 * x),
             (me + 1 - 2 * core, 4 * (1 - core), 3 - 2 * core, 1 + 2 * core),
         )
 
-    def peers(self):
-        near = [(self.steps[0][0], self.me >= 0), (self.steps[1][0], self.me >= 0)]
-        return near + self.others
-
-    def sent(self, step, piece):
-        other, source, there, _here = self.steps[step]
+    def copy(self, step, piece, arrived):
+        other, source, there, here = self.steps[step]
         return remote(
             self.buffer.at[source, piece],
-            self.buffer.at[there, piece],
+            self.buffer.at[here if arrived else there, piece],
             self.send.at[step, piece],
             self.recv.at[step, piece],
             other,
         )
 
+    def sent(self, step, piece):
+        return self.copy(step, piece, False)
+
     def arrived(self, step, piece):
-        other, source, _there, here = self.steps[step]
-        return remote(
-            self.buffer.at[source, piece],
-            self.buffer.at[here, piece],
-            self.send.at[step, piece],
-            self.recv.at[step, piece],
-            other,
-        )
+        return self.copy(step, piece, True)
 
     def start(self, piece):
         self.sent(0, piece).start()
 
     def forward(self, piece):
-        at = self.pieces.index(piece)
-        self.hand_on(at, at - 1, at - 2)
-
-    def hand_on(self, by_x, by_y, by_z):
-        late = self.x != self.core
-        if 0 <= by_x < len(self.pieces):
-            piece = self.pieces[by_x]
-            self.arrived(0, piece).wait_recv()
-            self.sent(2, piece).start()
-            pl.when(jnp.logical_not(late))(self.sent(4, piece).start)
-            self.sent(1, piece).start()
-        if 0 <= by_y < len(self.pieces):
-            piece = self.pieces[by_y]
-            self.arrived(2, piece).wait_recv()
-            pl.when(self.z_send)(self.sent(3, piece).start)
-            pl.when(jnp.logical_not(self.by_z) & late)(self.sent(4, piece).start)
-        if 0 <= by_z < len(self.pieces):
-            piece = self.pieces[by_z]
-
-            @pl.when(self.z_recv)
-            def _last():
-                self.arrived(3, piece).wait_recv()
-                pl.when(late)(self.sent(4, piece).start)
+        self.arrived(0, piece).wait_recv()
+        pl.when(self.onward)(self.sent(2, piece).start)
+        pl.when(jnp.logical_not(self.late))(self.sent(3, piece).start)
+        self.sent(1, piece).start()
 
     def finish(self):
-        late = self.x != self.core
-        for at in range(len(self.pieces), len(self.pieces) + 2):
-            self.hand_on(at, at - 1, at - 2)
+        for piece in self.pieces:
+
+            @pl.when(self.second)
+            def _second():
+                self.arrived(2, piece).wait_recv()
+                pl.when(self.late)(self.sent(3, piece).start)
+
         for piece in self.pieces:
             self.arrived(1, piece).wait_recv()
-            pl.when(self.second | late)(self.arrived(4, piece).wait_recv)
-            for step in range(3):
-                self.sent(step, piece).wait_send()
-            pl.when(self.z_send)(self.sent(3, piece).wait_send)
-            pl.when(self.second | jnp.logical_not(late))(self.sent(4, piece).wait_send)
-
-
-def way(count):
-    return Relay if count == 32 else Direct
+            pl.when(self.second | self.late)(self.arrived(3, piece).wait_recv)
+            self.sent(0, piece).wait_send()
+            self.sent(1, piece).wait_send()
+            pl.when(self.onward)(self.sent(2, piece).wait_send)
+            pl.when(self.second | jnp.logical_not(self.late))(self.sent(3, piece).wait_send)
 
 
 def faces_kernel(
@@ -249,11 +209,8 @@
 ):
     me = lax.axis_index("sfc")
     order = (4, 5, 0, 1, 2, 3)
-    faces = way(count)(me, count, near_ref, order, send, recv)
-    peers = direct_peers(me, count)
-    if count == 32:
-        peers = peers + faces.others
-    barrier, number = greet(me, peers)
+    faces = Relay(me, count, near_ref, order, send, recv)
+    barrier, number = greet(me, direct_peers(me, count) + faces.others)
 
     def extract_layers(slot, item, swap):
         for side in range(2):
@@ -344,8 +301,6 @@
     pl.semaphore_wait(barrier, number)
     for piece in pieces:
         packets.start(piece)
-    for piece in pieces:
-        packets.forward(piece)
     packets.finish()
 
 
@@ -373,7 +328,7 @@
 
 
 def fit(points, params):
-    width = 256
+    width = 128
 
     def normal_equations(start, params):
         a, b, c, d = [p[:, start : start + width] for p in params]
@@ -526,23 +481,26 @@
                 part % 4,
             )
 
-    for slot in range(refine_ref.shape[1]):
-        block = jnp.clip(refine_ref[0, slot] - me * BLK, 0, BLK - 1)
-        k = jnp.clip(refine_ref[1, slot], 0, 5)
-        yz = (k >= 2).astype(jnp.int32)
-        base = block * FINE_ROWS + yz * 8
-        group = k - 2 * yz
-        parts = []
-        for target in range(3):
-            if target < 2:
-                comp = (k // 2, 3)[target]
-                value = fine_table[pl.ds(pl.multiple_of(base + comp * 16, 8), 8), :]
-            else:
-                value = speed_ref[pl.ds(pl.multiple_of(block * 16 + yz * 8, 8), 8), :]
-            parts.append(pltpu.roll(value, (128 + 32 * target - 32 * group) % 128, 1))
-        packets_ref[slot] = jnp.where(
-            lane < 32, parts[0], jnp.where(lane < 64, parts[1], parts[2])
-        )
+    slots = refine_ref.shape[1]
+    for first in range(0, slots, 4):
+        whole = [jnp.zeros(VEC, jnp.float32)] * 3
+        for slot in range(first, min(first + 4, slots)):
+            block = jnp.clip(refine_ref[0, slot] - me * BLK, 0, BLK - 1)
+            k = jnp.clip(refine_ref[1, slot], 0, 5)
+            yz = (k >= 2).astype(jnp.int32)
+            base = block * FINE_ROWS + yz * 8
+            shift = (128 + 32 * (slot - first) - 32 * (k - 2 * yz)) % 128
+            values = [
+                fine_table[pl.ds(pl.multiple_of(base + comp * 16, 8), 8), :] for comp in (k // 2, 3)
+            ]
+            values.append(speed_ref[pl.ds(pl.multiple_of(block * 16 + yz * 8, 8), 8), :])
+            whole = [
+                jnp.where(lane // 32 == slot - first, pltpu.roll(value, shift, 1), other)
+                for value, other in zip(values, whole)
+            ]
+        for item in range(3):
+            start = (first // 4 * 3 + item) * 8
+            packets_ref[start : start + 8, :] = whole[item]
 
 
 def flux_kernel(faces_ref, speed_ref, packets_ref, table_ref, reflux_ref, live_list):
@@ -551,7 +509,7 @@
     row = lax.broadcasted_iota(jnp.int32, VEC, 0)
     pos = lane % 32
     cell = pos % 16 // 2
-    slots = packets_ref.shape[1]
+    slots = table_ref.shape[2]
 
     found = 0
     for offset in range(2 * REACH + 1):
@@ -600,10 +558,10 @@
             )
             for source in sources
         ]
-        packet = packets_ref[offset, slot]
-        normal_f = packet
-        d_f = pltpu.roll(packet, 96, 1)
-        u_f = pltpu.roll(packet, 64, 1)
+        back = (128 - 32 * (slot % 4)) % 128
+        normal_f, d_f, u_f = [
+            pltpu.roll(packets_ref[offset, slot // 4 * 3 + item], back, 1) for item in range(3)
+        ]
         speed = sign * 0.5 * (u_f + u_c)
         depth = jnp.abs(speed) * TIME_STEP
         outflow = jnp.maximum(speed, 0.0)
@@ -652,7 +610,7 @@
 def per_device(fraction, centroid, velocity, neighbours, refinement):
     count = lax.axis_size("sfc")
     slots = refinement.shape[0]
-    pieces = 4 if slots % 4 == 0 else 1
+    packet_rows = -(-slots // 4) * 3 * 8
     vmem, smem = spec(pltpu.VMEM), spec(pltpu.SMEM)
     f32 = jnp.float32
     refinement = refinement.T
@@ -661,13 +619,13 @@
     near, table, speeds = pl.pallas_call(
         lambda *refs: faces_kernel(count, *refs),
         out_shape=(
-            jax.ShapeDtypeStruct((7, ITEMS, BLK * 8, 128), f32),
+            jax.ShapeDtypeStruct((6, ITEMS, BLK * 8, 128), f32),
             jax.ShapeDtypeStruct((5, 4, slots), jnp.int32),
             jax.ShapeDtypeStruct((BLK * 16, 128), f32),
         ),
         in_specs=[vmem] * 5,
         out_specs=(vmem,) * 3,
-        scratch_shapes=[pltpu.SemaphoreType.DMA((5, ITEMS))] * 2
+        scratch_shapes=[pltpu.SemaphoreType.DMA((4, ITEMS))] * 2
         + [pltpu.SemaphoreType.DMA((4,))] * 2,
         compiler_params=pltpu.CompilerParams(collective_id=0, has_side_effects=True),
         name="exchange_faces",
@@ -677,7 +635,7 @@
         out_shape=(
             jax.ShapeDtypeStruct((BLK, 4, CELLS), f32),
             jax.ShapeDtypeStruct((BLK * FINE_ROWS, 128), f32),
-            jax.ShapeDtypeStruct((slots, 8, 128), f32),
+            jax.ShapeDtypeStruct((packet_rows, 128), f32),
         ),
         in_specs=[vmem] * 6 + [smem] * 2,
         out_specs=(vmem,) * 3,
@@ -695,19 +653,19 @@
         speeds,
         edge,
         ghost_matrix(),
-        near.reshape(7, ITEMS, BLK, 8, 128),
+        near.reshape(6, ITEMS, BLK, 8, 128),
         neighbours,
         refinement,
     )
     near_packets = pl.pallas_call(
         lambda *refs: packets_kernel(count, *refs),
-        out_shape=jax.ShapeDtypeStruct((7, pieces, slots // pieces * 8, 128), f32),
+        out_shape=jax.ShapeDtypeStruct((5, 1, packet_rows, 128), f32),
         in_specs=[vmem],
         out_specs=vmem,
-        scratch_shapes=[pltpu.SemaphoreType.DMA((5, pieces))] * 2,
+        scratch_shapes=[pltpu.SemaphoreType.DMA((4, 1))] * 2,
         compiler_params=pltpu.CompilerParams(collective_id=1, has_side_effects=True),
         name="exchange_packets",
-    )(packets.reshape(pieces, slots // pieces * 8, 128))
+    )(packets.reshape(1, packet_rows, 128))
     reflux = pl.pallas_call(
         flux_kernel,
         out_shape=jax.ShapeDtypeStruct((BLK, 6, 2, 256), f32),
@@ -715,7 +673,7 @@
         out_specs=vmem,
         scratch_shapes=[pltpu.SMEM((5 * slots + 4,), jnp.int32)],
         name="reflux_moments",
-    )(faces, speeds, near_packets.reshape(7, slots, 8, 128), table)
+    )(faces, speeds, near_packets.reshape(5, packet_rows // 8, 8, 128), table)
     return planes, reflux
 
 

time: 54.6 us -> 43 us (0.79)
  the two profiles are of different devices: /device:TPU:11 before, /device:TPU:0 now
where the time goes in v5:
time: 43 us; the launch traced here: 42.8 us
  Pallas kernels  42.2 us (98%)
  between operations  0.65 us (2%)
    pallas_call x1, Pallas kernels, per_device(): pl.pallas_call(fit_kernel, out_shape=(jax.ShapeDtypeStruct((BLK, 4, CELLS...  14.6 us
    pallas_call x1, Pallas kernels, per_device(): pl.pallas_call(lambda *refs: faces_kernel(count, *refs), out_shape=(jax.S...  14.1 us
    pallas_call x1, Pallas kernels, per_device(): pl.pallas_call(lambda *refs: packets_kernel(count, *refs), out_shape=jax....  9.52 us
    pallas_call x1, Pallas kernels, per_device(): pl.pallas_call(flux_kernel, out_shape=jax.ShapeDtypeStruct((BLK, 6, 2, 25...  4.01 us

profile of v5, /device:TPU:0, one launch (start us, length us, event | category | flops | bytes accessed | tf_op | source)
XLA Modules:
  0.0 42.8 jit_solution(1879823805464069015)
XLA Ops:
  0.6 14.1 %exchange_faces.1 = (f32[6,6,64,128]{3,2,1,0:T(8,128)}, s32[5,4,16]{2,1,0:T(4,128)}, f32[128,128]{1,0:T(8,128)}) custom-call(f32[8,4096]{1,0:T(8,128)} %fraction_ref.1, f32[3,8,4096]{2,1,0:T(8,128)} %bitcast.6, f32[3,8,4096]{2,1,0:T(8,128)} %bitcast.10, s32[4,16]{1,0:T(4,128)} %bitcast.12, bf16[512,256]{1,0:T(8,128)(2,1)} %constant.4.clone.refs_4_.edge_ref), custom_call_target="tpu_custom_call" | custom-call | tf_op jit(solution)/shard_map/exchange_faces/pallas_call | solution.py:619
  14.7 14.6 %fit_planes.1 = (f32[8,4,4096]{2,1,0:T(4,128)}, f32[512,128]{1,0:T(8,128)}, f32[96,128]{1,0:T(8,128)}) custom-call(f32[8,4096]{1,0:T(8,128)} %fraction_ref.1, f32[3,8,4096]{2,1,0:T(8,128)} %bitcast.7, f32[128,128]{1,0:T(8,128)} %get-tuple-element.8.speed_ref, bf16[512,256]{1,0:T(8,128)(2,1)} %constant.4.clone.refs_4_.edge_ref, ...), custom_call_target="tpu_custom_call" | custom-call | tf_op jit(solution)/shard_map/fit_planes/pallas_call | solution.py:633
  29.3 9.5 %exchange_packets.1 = f32[5,1,96,128]{3,2,1,0:T(8,128)} custom-call(f32[1,96,128]{2,1,0:T(8,128)} %bitcast.11), custom_call_target="tpu_custom_call" | custom-call | tf_op jit(solution)/shard_map/exchange_packets/pallas_call | solution.py:660
  38.8 4.0 %reflux_moments.1 = f32[8,6,2,256]{3,2,1,0:T(2,128)} custom-call(f32[512,128]{1,0:T(8,128)} %get-tuple-element.11.faces_ref, f32[128,128]{1,0:T(8,128)} %get-tuple-element.8.speed_ref, f32[5,12,8,128]{3,2,1,0:T(8,128)} %bitcast.9, s32[5,4,16]{2,1,0:T(4,128)} %get-tuple-element.13.table_ref), custom_call_target="tpu_custom_call" | custom-call | tf_op jit(solution)/shard_map/reflux_moments/pallas_call | solution.py:669

commit v6 on v5

--- a/solution.py
+++ b/solution.py
@@ -356,7 +356,7 @@
         return h + g
 
     def one_pass(_unused, params):
-        parts = [normal_equations(start, params) for start in range(0, 512, width)]
+        parts = [normal_equations(start, params) for start in range(0, params[0].shape[1], width)]
         sums = [jnp.concatenate(part, 1) for part in zip(*parts)]
         step = solve(sums[:10], sums[10:])
         return tuple(p - s for p, s in zip(params, step))
@@ -432,7 +432,7 @@
         shifts = (0, 80, 112, 64)
         return jnp.concatenate([pltpu.roll(ghost, i, 1) if i else ghost for i in shifts], 1)
 
-    def one_pair(pair, carry):
+    def stencil(pair):
         start = pl.multiple_of(pair * 512, 512)
         fields = [[] for _unused in range(7)]
         for field in range(4):
@@ -457,13 +457,29 @@
             f, *coords = fields[k + 1]
             coords[k // 2] = coords[k // 2] + (2.0 * (k % 2) - 1.0)
             points.append((*coords, 2.0 * f - 1.0))
-        params = fit(points, (a, b, c, d))
-        for comp in range(4):
-            planes_ref[:, comp, pl.ds(start, 512)] = params[comp]
-            layers[pl.ds(pl.multiple_of(pair * 32 + comp * 8, 8), 8), :] = params[comp]
+        return points, (a, b, c, d)
+
+    together = 2
+
+    def some_pairs(number, carry):
+        pairs = [number * together + i for i in range(together)]
+        stencils = [stencil(pair) for pair in pairs]
+        points = [
+            tuple(jnp.concatenate(values, 1) for values in zip(*same))
+            for same in zip(*[points for points, _unused in stencils])
+        ]
+        params = fit(
+            points, tuple(jnp.concatenate(values, 1) for values in zip(*[p for _unused, p in stencils]))
+        )
+        for i, pair in enumerate(pairs):
+            start = pl.multiple_of(pair * 512, 512)
+            for comp in range(4):
+                value = params[comp][:, i * 512 : i * 512 + 512]
+                planes_ref[:, comp, pl.ds(start, 512)] = value
+                layers[pl.ds(pl.multiple_of(pair * 32 + comp * 8, 8), 8), :] = value
         return carry
 
-    lax.fori_loop(0, 8, one_pair, 0)
+    lax.fori_loop(0, 8 // together, some_pairs, 0)
 
     edge_values = select(layers[...], edge_ref[:, 128:])
     for pair in range(8):

time: 43 us -> 42.4 us (0.986)
  Pallas kernels: 42.2 us -> 41.6 us
    pallas_call x1, Pallas kernels: 14.6 us -> 14 us  [per_device(): pl.pallas_call(fit_kernel, out_shape=(jax.ShapeDtypeStruct((BLK, 4, CELLS...]
where the time goes in v6:
time: 42.4 us; the launch traced here: 42.3 us
  Pallas kernels  41.6 us (98%)
  between operations  0.65 us (2%)
    pallas_call x1, Pallas kernels, per_device(): pl.pallas_call(lambda *refs: faces_kernel(count, *refs), out_shape=(jax.S...  14.1 us
    pallas_call x1, Pallas kernels, per_device(): pl.pallas_call(fit_kernel, out_shape=(jax.ShapeDtypeStruct((BLK, 4, CELLS...  14 us
    pallas_call x1, Pallas kernels, per_device(): pl.pallas_call(lambda *refs: packets_kernel(count, *refs), out_shape=jax....  9.52 us
    pallas_call x1, Pallas kernels, per_device(): pl.pallas_call(flux_kernel, out_shape=jax.ShapeDtypeStruct((BLK, 6, 2, 25...  4.01 us

profile of v6, /device:TPU:0, one launch (start us, length us, event | category | flops | bytes accessed | tf_op | source)
XLA Modules:
  0.0 42.3 jit_solution(14422034469816045208)
XLA Ops:
  0.6 14.1 %exchange_faces.1 = (f32[6,6,64,128]{3,2,1,0:T(8,128)}, s32[5,4,16]{2,1,0:T(4,128)}, f32[128,128]{1,0:T(8,128)}) custom-call(f32[8,4096]{1,0:T(8,128)} %fraction_ref.1, f32[3,8,4096]{2,1,0:T(8,128)} %bitcast.6, f32[3,8,4096]{2,1,0:T(8,128)} %bitcast.10, s32[4,16]{1,0:T(4,128)} %bitcast.12, bf16[512,256]{1,0:T(8,128)(2,1)} %constant.4.clone.refs_4_.edge_ref), custom_call_target="tpu_custom_call" | custom-call | tf_op jit(solution)/shard_map/exchange_faces/pallas_call | solution.py:635
  14.7 14.0 %fit_planes.1 = (f32[8,4,4096]{2,1,0:T(4,128)}, f32[512,128]{1,0:T(8,128)}, f32[96,128]{1,0:T(8,128)}) custom-call(f32[8,4096]{1,0:T(8,128)} %fraction_ref.1, f32[3,8,4096]{2,1,0:T(8,128)} %bitcast.7, f32[128,128]{1,0:T(8,128)} %get-tuple-element.8.speed_ref, bf16[512,256]{1,0:T(8,128)(2,1)} %constant.4.clone.refs_4_.edge_ref, ...), custom_call_target="tpu_custom_call" | custom-call | tf_op jit(solution)/shard_map/fit_planes/pallas_call | solution.py:649
  28.7 9.5 %exchange_packets.1 = f32[5,1,96,128]{3,2,1,0:T(8,128)} custom-call(f32[1,96,128]{2,1,0:T(8,128)} %bitcast.11), custom_call_target="tpu_custom_call" | custom-call | tf_op jit(solution)/shard_map/exchange_packets/pallas_call | solution.py:676
  38.3 4.0 %reflux_moments.1 = f32[8,6,2,256]{3,2,1,0:T(2,128)} custom-call(f32[512,128]{1,0:T(8,128)} %get-tuple-element.11.faces_ref, f32[128,128]{1,0:T(8,128)} %get-tuple-element.8.speed_ref, f32[5,12,8,128]{3,2,1,0:T(8,128)} %bitcast.9, s32[5,4,16]{2,1,0:T(4,128)} %get-tuple-element.13.table_ref), custom_call_target="tpu_custom_call" | custom-call | tf_op jit(solution)/shard_map/reflux_moments/pallas_call | solution.py:685

commit v7 on v6

--- a/solution.py
+++ b/solution.py
@@ -222,6 +222,24 @@
 
     extract_layers(REACH, 4, True)
     extract_layers(REACH, 5, True)
+    speeds = select(
+        jnp.concatenate(
+            [velocity_ref[axis, :, pl.ds(pair * 512, 512)] for axis in (1, 2) for pair in range(8)],
+            0,
+        ),
+        edge_ref[:, 128:],
+    )
+    for pair in range(8):
+        speed_ref[pl.ds(8 + pair, 8, stride=16), :] = jnp.where(
+            lanes() < 64, speeds[pair * 8 : pair * 8 + 8], speeds[64 + pair * 8 : 72 + pair * 8]
+        )
+    for part in range(8):
+        start = part // 4 * 128
+        speed_ref[pl.ds(part, 8, stride=16), :] = layer_parts(
+            velocity_ref[0, :, start : start + 128],
+            velocity_ref[0, :, 3840 + start : 3968 + start],
+            part % 4,
+        )
     pl.semaphore_wait(barrier, number)
     faces.start(4)
     faces.start(5)
@@ -265,25 +283,7 @@
     faces.forward(4)
     faces.forward(5)
     faces.forward(0)
-    speeds = select(
-        jnp.concatenate(
-            [velocity_ref[axis, :, pl.ds(pair * 512, 512)] for axis in (1, 2) for pair in range(8)],
-            0,
-        ),
-        edge_ref[:, 128:],
-    )
-    for pair in range(8):
-        speed_ref[pl.ds(8 + pair, 8, stride=16), :] = jnp.where(
-            lanes() < 64, speeds[pair * 8 : pair * 8 + 8], speeds[64 + pair * 8 : 72 + pair * 8]
-        )
     faces.forward(1)
-    for part in range(8):
-        start = part // 4 * 128
-        speed_ref[pl.ds(part, 8, stride=16), :] = layer_parts(
-            velocity_ref[0, :, start : start + 128],
-            velocity_ref[0, :, 3840 + start : 3968 + start],
-            part % 4,
-        )
     faces.forward(2)
     faces.forward(3)
     faces.finish()
@@ -459,7 +459,7 @@
             points.append((*coords, 2.0 * f - 1.0))
         return points, (a, b, c, d)
 
-    together = 2
+    together = 4
 
     def some_pairs(number, carry):
         pairs = [number * together + i for i in range(together)]

time: 42.4 us -> 42.9 us (1.012)
  Pallas kernels: 41.6 us -> 42.1 us
    pallas_call x1, Pallas kernels: 14 us -> 14.5 us  [per_device(): pl.pallas_call(fit_kernel, out_shape=(jax.ShapeDtypeStruct((BLK, 4, CELLS...]
where the time goes in v7:
time: 42.9 us; the launch traced here: 42.7 us
  Pallas kernels  42.1 us (98%)
  between operations  0.65 us (2%)
    pallas_call x1, Pallas kernels, per_device(): pl.pallas_call(fit_kernel, out_shape=(jax.ShapeDtypeStruct((BLK, 4, CELLS...  14.5 us
    pallas_call x1, Pallas kernels, per_device(): pl.pallas_call(lambda *refs: faces_kernel(count, *refs), out_shape=(jax.S...  14.1 us
    pallas_call x1, Pallas kernels, per_device(): pl.pallas_call(lambda *refs: packets_kernel(count, *refs), out_shape=jax....  9.52 us
    pallas_call x1, Pallas kernels, per_device(): pl.pallas_call(flux_kernel, out_shape=jax.ShapeDtypeStruct((BLK, 6, 2, 25...  4.01 us

profile of v7, /device:TPU:0, one launch (start us, length us, event | category | flops | bytes accessed | tf_op | source)
XLA Modules:
  0.0 42.7 jit_solution(12423202664701780786)
XLA Ops:
  0.6 14.1 %exchange_faces.1 = (f32[6,6,64,128]{3,2,1,0:T(8,128)}, s32[5,4,16]{2,1,0:T(4,128)}, f32[128,128]{1,0:T(8,128)}) custom-call(f32[8,4096]{1,0:T(8,128)} %fraction_ref.1, f32[3,8,4096]{2,1,0:T(8,128)} %bitcast.6, f32[3,8,4096]{2,1,0:T(8,128)} %bitcast.10, s32[4,16]{1,0:T(4,128)} %bitcast.12, bf16[512,256]{1,0:T(8,128)(2,1)} %constant.4.clone.refs_4_.edge_ref), custom_call_target="tpu_custom_call" | custom-call | tf_op jit(solution)/shard_map/exchange_faces/pallas_call | solution.py:635
  14.7 14.5 %fit_planes.1 = (f32[8,4,4096]{2,1,0:T(4,128)}, f32[512,128]{1,0:T(8,128)}, f32[96,128]{1,0:T(8,128)}) custom-call(f32[8,4096]{1,0:T(8,128)} %fraction_ref.1, f32[3,8,4096]{2,1,0:T(8,128)} %bitcast.7, f32[128,128]{1,0:T(8,128)} %get-tuple-element.8.speed_ref, bf16[512,256]{1,0:T(8,128)(2,1)} %constant.4.clone.refs_4_.edge_ref, ...), custom_call_target="tpu_custom_call" | custom-call | tf_op jit(solution)/shard_map/fit_planes/pallas_call | solution.py:649
  29.2 9.5 %exchange_packets.1 = f32[5,1,96,128]{3,2,1,0:T(8,128)} custom-call(f32[1,96,128]{2,1,0:T(8,128)} %bitcast.11), custom_call_target="tpu_custom_call" | custom-call | tf_op jit(solution)/shard_map/exchange_packets/pallas_call | solution.py:676
  38.7 4.0 %reflux_moments.1 = f32[8,6,2,256]{3,2,1,0:T(2,128)} custom-call(f32[512,128]{1,0:T(8,128)} %get-tuple-element.11.faces_ref, f32[128,128]{1,0:T(8,128)} %get-tuple-element.8.speed_ref, f32[5,12,8,128]{3,2,1,0:T(8,128)} %bitcast.9, s32[5,4,16]{2,1,0:T(4,128)} %get-tuple-element.13.table_ref), custom_call_target="tpu_custom_call" | custom-call | tf_op jit(solution)/shard_map/reflux_moments/pallas_call | solution.py:685
